TPU v7x, 32 devices: a whole 2x2x4 slice. The times are simulated.
32 devices in a mesh: section: 4 (over y, core), dp: 8 (over z, x).
Axes of the slice: x: 2, y: 2, z: 4, core: 2. Of those that a mesh axis runs over, the one named last changes fastest.
Arguments:
- hidden_in: bfloat16 [4, 256, 8192], P(None, 'dp'), may hold values from -6 to 6
- cotangent: bfloat16 [4, 256, 8192], P(None, 'dp'), may hold values from -6 to 6
- adapter_in: bfloat16 [4, 8192, 128], P('section', 'dp'), may hold values from -0.0625 to 0.0625
- adapter_out: bfloat16 [4, 128, 8192], P('section', None, 'dp'), may hold values from -0.5 to 0.5
- norm_gain: bfloat16 [4, 8192], P('section', 'dp'), may hold values from 0.5 to 1.5
- user_of_row: int32 [4, 256], P(None, 'dp'), may hold values from 0 to 15, as said below
- included: int32 [4, 16], P(None, 'dp'), may hold values 0 or 1
Outputs:
- grad_in: float32 [4, 8192, 128], P('section', 'dp')
- grad_out: float32 [4, 128, 8192], P('section', None, 'dp')
- user_weights: float32 [4, 16], P(None, 'dp')
Inputs may be any that keep to these rules, and one draw needn't show every extreme that they name: `user_of_row`: within one micro-batch, the rows of the j-th block of 32 rows belong to users j * 2 to j * 2 + 1, in rising order, each of them with one row or more.
All inputs are finite; a program needn't handle non-finite values. No bound on the sum of `included` on one device may be relied on, other than what follows from the above.
Results may differ from a plain program's by a relative error of at most 0.018.
Values may be sent and summed in bfloat16 or wider, within the bound.
No kernel may reach another device: no remote copies, remote signals or barrier semaphores. Data moves between devices by JAX's collectives and lax.ppermute only.
A program may use at most 64 MiB of HBM per device.

v0:
```python
import math

import jax
import jax.numpy as jnp
from jax import lax
from jax.sharding import PartitionSpec as P


def from_behind(block, axis, distance):
    devices = range(lax.axis_size(axis))
    route = [(i - distance, i) for i in devices if i - distance in devices]
    return lax.ppermute(block, axis, route)


def normalize(stream_in, gain):
    stream = stream_in.astype(jnp.float32)
    scale = lax.rsqrt(jnp.mean(stream * stream, -1, keepdims=True) + 1e-05)
    unit = stream * scale
    normed = (unit * gain).astype(jnp.bfloat16)
    return (stream, scale, unit, normed)


def place(store, value, index, active):
    old = lax.dynamic_index_in_dim(store, index, 0, keepdims=False)
    return lax.dynamic_update_index_in_dim(store, jnp.where(active, value, old), index, 0)


def contract_last(left, right):
    return lax.dot_general(
        left, right, (((1,), (1,)), ((), ())), preferred_element_type=jnp.float32
    )


def contract_first(left, right):
    return lax.dot_general(
        left, right, (((0,), (0,)), ((), ())), preferred_element_type=jnp.float32
    )


def ghost(normed, err, low, delta, owners, onehot):
    same = owners[:, None] == owners[None, :]
    pairs = contract_last(normed, normed) * contract_last(err, err) + contract_last(
        low, low
    ) * contract_last(delta, delta)
    pairs = jnp.where(same, pairs, jnp.zeros_like(pairs))
    return jnp.sum(onehot * jnp.sum(pairs, -1)[:, None], 0)


def shards(hidden_in, cotangent, adapter_in, adapter_out, norm_gain, user_of_row, included):
    sections = lax.axis_size("section")
    section = lax.axis_index("section")
    dp_index = lax.axis_index("dp")
    a_full, b_full, g_full = (
        lax.all_gather(adapter_in, "dp", axis=1, tiled=True),
        lax.all_gather(adapter_out, "dp", axis=2, tiled=True),
        lax.all_gather(norm_gain, "dp", axis=1, tiled=True),
    )
    a_mat = a_full[0]
    b_mat = b_full[0]
    gain = g_full[0].astype(jnp.float32)
    micro, rows, width = hidden_in.shape
    rank = a_mat.shape[1]
    users = included.shape[1]
    ticks = micro + sections - 1
    local_ids = user_of_row - dp_index * users
    onehot = (local_ids[:, :, None] == jnp.arange(users, dtype=jnp.int32)[None, None, :]).astype(
        jnp.float32
    )

    def forward_tick(carry, tick):
        incoming, keep_h, keep_n, keep_z = carry
        slot = tick - section
        active = (slot >= 0) & (slot < micro)
        index = jnp.clip(slot, 0, micro - 1)
        source = lax.dynamic_index_in_dim(hidden_in, index, 0, keepdims=False)
        current = jnp.where(section == 0, source, incoming)
        stream, scale, unit, normed = normalize(current, gain)
        low = jnp.dot(normed, a_mat, preferred_element_type=jnp.float32).astype(jnp.bfloat16)
        result = (stream + jnp.dot(low, b_mat, preferred_element_type=jnp.float32)).astype(
            jnp.bfloat16
        )
        keep_h = place(keep_h, current, index, active)
        keep_n = place(keep_n, normed, index, active)
        keep_z = place(keep_z, low, index, active)
        outgoing = from_behind(result, "section", 1)
        return ((outgoing, keep_h, keep_n, keep_z), None)

    start_fwd = (
        jnp.zeros((rows, width), jnp.bfloat16),
        jnp.zeros_like(hidden_in),
        jnp.zeros_like(hidden_in),
        jnp.zeros((micro, rows, rank), jnp.bfloat16),
    )
    (unused, keep_h, keep_n, keep_z), unused_out = lax.scan(
        forward_tick, start_fwd, jnp.arange(ticks, dtype=jnp.int32)
    )

    def backward_tick(carry, tick):
        incoming, carried, keep_e, keep_d, keep_p = carry
        slot = tick - (sections - 1 - section)
        active = (slot >= 0) & (slot < micro)
        index = jnp.clip(slot, 0, micro - 1)
        source = lax.dynamic_index_in_dim(cotangent, index, 0, keepdims=False)
        delta = jnp.where(section == sections - 1, source, incoming)
        current = lax.dynamic_index_in_dim(keep_h, index, 0, keepdims=False)
        normed = lax.dynamic_index_in_dim(keep_n, index, 0, keepdims=False)
        low = lax.dynamic_index_in_dim(keep_z, index, 0, keepdims=False)
        owners = lax.dynamic_index_in_dim(user_of_row, index, 0, keepdims=False)
        hot = lax.dynamic_index_in_dim(onehot, index, 0, keepdims=False)
        stream, scale, unit, unused_n = normalize(current, gain)
        err = contract_last(delta, b_mat).astype(jnp.bfloat16)
        slope = contract_last(err, a_mat) * gain
        grad_h = scale * (slope - unit * jnp.mean(slope * unit, -1, keepdims=True))
        previous = (delta.astype(jnp.float32) + grad_h).astype(jnp.bfloat16)
        partial_value = ghost(normed, err, low, delta, owners, hot)
        keep_e = place(keep_e, err, index, active)
        keep_d = place(keep_d, delta, index, active)
        keep_p = place(keep_p, partial_value, index, active)
        outgoing = from_behind(previous, "section", -1)
        return ((outgoing, carried, keep_e, keep_d, keep_p), None)

    start_bwd = (
        jnp.zeros((rows, width), jnp.bfloat16),
        jnp.zeros((users,), jnp.float32),
        jnp.zeros((micro, rows, rank), jnp.bfloat16),
        jnp.zeros_like(cotangent),
        jnp.zeros((micro, users), jnp.float32),
    )
    (unused_a, unused_b, keep_e, keep_d, keep_p), unused_out = lax.scan(
        backward_tick, start_bwd, jnp.arange(ticks, dtype=jnp.int32)
    )
    total = lax.psum(keep_p, "section")
    bound = 0.8 * math.sqrt(sections * (rows // users) * width * width)
    user_weights = included.astype(jnp.float32) * (bound / jnp.maximum(jnp.sqrt(total), bound))
    row_weight = jnp.sum(onehot * user_weights[:, None, :], -1)[:, :, None]
    weighted_err = (
        (row_weight * keep_e.astype(jnp.float32)).astype(jnp.bfloat16).reshape(micro * rows, rank)
    )
    weighted_delta = (
        (row_weight * keep_d.astype(jnp.float32)).astype(jnp.bfloat16).reshape(micro * rows, width)
    )
    normed_rows = keep_n.reshape(micro * rows, width)
    low_rows = keep_z.reshape(micro * rows, rank)
    shard = lax.psum_scatter(
        jnp.concatenate(
            [contract_first(normed_rows, weighted_err), contract_first(weighted_delta, low_rows)], 1
        ).astype(jnp.bfloat16),
        "dp",
        scatter_dimension=0,
        tiled=True,
    ).astype(jnp.float32)
    grad_in = shard[:, :rank]
    grad_out = shard[:, rank:].T
    return (grad_in[None], grad_out[None], user_weights)


def solution(mesh):
    placed = (
        P(None, "dp", None),
        P(None, "dp", None),
        P("section", "dp", None),
        P("section", None, "dp"),
        P("section", "dp"),
        P(None, "dp"),
        P(None, "dp"),
    )
    return jax.shard_map(
        shards,
        mesh=mesh,
        in_specs=placed,
        out_specs=(P("section", "dp", None), P("section", None, "dp"), P(None, "dp")),
        check_vma=False,
    )
```

profile of v0, /device:TPU:0, one launch (start us, length us, event | category | flops | bytes accessed | tf_op | source)
XLA Modules:
  0.0 472.1 jit_solution(13993370653413089227)
XLA Ops:
  8.7 32.4 %all_gather.9 = bf16[1,8192]{1,0:T(2,128)(2,1)S(1)} all-gather(bf16[1,1024]{1,0:T(2,128)(2,1)} %param.15), channel_id=1, replica_groups=mesh['section'=4,'dp'=8] {'dp'}, dimensions={1}, use_global_device_ids=true | all-gather | bytes 18432 | tf_op jit(solution)/shard_map/all_gather | solution.py:56
  41.9 20.3 %all-gather.3.cloned.1.call-done = bf16[1,8192,128]{2,1,0:T(8,128)(2,1)} async-done(((bf16[1,1024,128]{2,1,0:T(8,128)(2,1)}), bf16[1,8192,128]{2,1,0:T(8,128)(2,1)}) %all-gather.3.cloned.1.call-update) | async-done | bytes 2097168 | tf_op jit(solution)/shard_map/all_gather | solution.py:54
  62.2 50.0 %all-gather.5.cloned.1.call-done = bf16[1,128,8192]{2,1,0:T(8,128)(2,1)} async-done(((bf16[1,128,1024]{2,1,0:T(8,128)(2,1)}), bf16[1,128,8192]{2,1,0:T(8,128)(2,1)}) %all-gather.5.cloned.1.call-update) | async-done | bytes 2097168 | tf_op jit(solution)/shard_map/all_gather | solution.py:55
  115.3 110.1 %while.35 = (s32[]{:T(128)}, bf16[32,8192]{1,0:T(8,128)(2,1)S(1)}, bf16[4,32,8192]{2,1,0:T(8,128)(2,1)}, bf16[4,32,8192]{2,1,0:T(8,128)(2,1)}, bf16[4,32,128]{2,...) while((s32[]{:T(128)}, bf16[32,8192]{1,0:T(8,128)(2,1)S(1)}, ...), condition=%wide.region_2.3_spmd, body=%wide.region_0.2_spmd.sunk | while | flops 138682400 | bytes 23185208 | solution.py:94
  131.4 8.0 %collective-permute-start = (bf16[32,8192]{1,0:T(8,128)(2,1)S(1)}, bf16[32,8192]{1,0:T(8,128)(2,1)S(1)}, u32[]{:S(2)}, u32[]{:S(2)}) collective-permute-start(bf16[32,8192]{1,0:T(8,128)(2,1)S(1)} %fusion.73), channel_id=1, source_target_pairs={{0,8},{8,16},{16,24},{1,9},{9,17},{17,25},{2,10},{10,18},{18,26},{... | collective-permute-start | bytes 1572872 | tf_op jit(solution)/shard_map/while/body/eval_jaxpr/ppermute | solution.py:12
  147.9 8.3 %collective-permute-start = (bf16[32,8192]{1,0:T(8,128)(2,1)S(1)}, bf16[32,8192]{1,0:T(8,128)(2,1)S(1)}, u32[]{:S(2)}, u32[]{:S(2)}) collective-permute-start(bf16[32,8192]{1,0:T(8,128)(2,1)S(1)} %fusion.73), channel_id=1, source_target_pairs={{0,8},{8,16},{16,24},{1,9},{9,17},{17,25},{2,10},{10,18},{18,26},{... | collective-permute-start | bytes 1572872 | tf_op jit(solution)/shard_map/while/body/eval_jaxpr/ppermute | solution.py:12
  164.6 8.4 %collective-permute-start = (bf16[32,8192]{1,0:T(8,128)(2,1)S(1)}, bf16[32,8192]{1,0:T(8,128)(2,1)S(1)}, u32[]{:S(2)}, u32[]{:S(2)}) collective-permute-start(bf16[32,8192]{1,0:T(8,128)(2,1)S(1)} %fusion.73), channel_id=1, source_target_pairs={{0,8},{8,16},{16,24},{1,9},{9,17},{17,25},{2,10},{10,18},{18,26},{... | collective-permute-start | bytes 1572872 | tf_op jit(solution)/shard_map/while/body/eval_jaxpr/ppermute | solution.py:12
  181.4 8.3 %collective-permute-start = (bf16[32,8192]{1,0:T(8,128)(2,1)S(1)}, bf16[32,8192]{1,0:T(8,128)(2,1)S(1)}, u32[]{:S(2)}, u32[]{:S(2)}) collective-permute-start(bf16[32,8192]{1,0:T(8,128)(2,1)S(1)} %fusion.73), channel_id=1, source_target_pairs={{0,8},{8,16},{16,24},{1,9},{9,17},{17,25},{2,10},{10,18},{18,26},{... | collective-permute-start | bytes 1572872 | tf_op jit(solution)/shard_map/while/body/eval_jaxpr/ppermute | solution.py:12
  198.2 8.3 %collective-permute-start = (bf16[32,8192]{1,0:T(8,128)(2,1)S(1)}, bf16[32,8192]{1,0:T(8,128)(2,1)S(1)}, u32[]{:S(2)}, u32[]{:S(2)}) collective-permute-start(bf16[32,8192]{1,0:T(8,128)(2,1)S(1)} %fusion.73), channel_id=1, source_target_pairs={{0,8},{8,16},{16,24},{1,9},{9,17},{17,25},{2,10},{10,18},{18,26},{... | collective-permute-start | bytes 1572872 | tf_op jit(solution)/shard_map/while/body/eval_jaxpr/ppermute | solution.py:12
  214.9 8.3 %collective-permute-start = (bf16[32,8192]{1,0:T(8,128)(2,1)S(1)}, bf16[32,8192]{1,0:T(8,128)(2,1)S(1)}, u32[]{:S(2)}, u32[]{:S(2)}) collective-permute-start(bf16[32,8192]{1,0:T(8,128)(2,1)S(1)} %fusion.73), channel_id=1, source_target_pairs={{0,8},{8,16},{16,24},{1,9},{9,17},{17,25},{2,10},{10,18},{18,26},{... | collective-permute-start | bytes 1572872 | tf_op jit(solution)/shard_map/while/body/eval_jaxpr/ppermute | solution.py:12
  227.0 129.4 %while.36 = (s32[]{:T(128)}, bf16[32,8192]{1,0:T(8,128)(2,1)S(1)}, bf16[4,32,128]{2,1,0:T(8,128)(2,1)S(1)}, bf16[4,32,8192]{2,1,0:T(8,128)(2,1)}, f32[4,2]{1,0:T...) while((s32[]{:T(128)}, bf16[32,8192]{1,0:T(8,128)(2,1)S(1)}, ...), condition=%wide.region_8.9_spmd, body=%wide.region_3.8_spmd.sunk | while | flops 173029504 | bytes 33156040 | solution.py:129
  239.2 5.5 %collective-permute-done.1 = bf16[32,8192]{1,0:T(8,128)(2,1)S(1)} collective-permute-done((bf16[32,8192]{1,0:T(8,128)(2,1)S(1)}, bf16[32,8192]{1,0:T(8,128)(2,1)S(1)}, u32[]{:S(2)}, u32[]{:S(2)}) %collective-permute-start.1) | collective-permute-done | bytes 524320 | tf_op jit(solution)/shard_map/while/body/eval_jaxpr/ppermute | solution.py:12
  256.9 7.1 %collective-permute-done.1 = bf16[32,8192]{1,0:T(8,128)(2,1)S(1)} collective-permute-done((bf16[32,8192]{1,0:T(8,128)(2,1)S(1)}, bf16[32,8192]{1,0:T(8,128)(2,1)S(1)}, u32[]{:S(2)}, u32[]{:S(2)}) %collective-permute-start.1) | collective-permute-done | bytes 524320 | tf_op jit(solution)/shard_map/while/body/eval_jaxpr/ppermute | solution.py:12
  276.1 6.3 %collective-permute-done.1 = bf16[32,8192]{1,0:T(8,128)(2,1)S(1)} collective-permute-done((bf16[32,8192]{1,0:T(8,128)(2,1)S(1)}, bf16[32,8192]{1,0:T(8,128)(2,1)S(1)}, u32[]{:S(2)}, u32[]{:S(2)}) %collective-permute-start.1) | collective-permute-done | bytes 524320 | tf_op jit(solution)/shard_map/while/body/eval_jaxpr/ppermute | solution.py:12
  294.6 6.3 %collective-permute-done.1 = bf16[32,8192]{1,0:T(8,128)(2,1)S(1)} collective-permute-done((bf16[32,8192]{1,0:T(8,128)(2,1)S(1)}, bf16[32,8192]{1,0:T(8,128)(2,1)S(1)}, u32[]{:S(2)}, u32[]{:S(2)}) %collective-permute-start.1) | collective-permute-done | bytes 524320 | tf_op jit(solution)/shard_map/while/body/eval_jaxpr/ppermute | solution.py:12
  304.6 2.2 bitcast_dynamic-update-slice_fusion.13
  313.2 6.2 %collective-permute-done.1 = bf16[32,8192]{1,0:T(8,128)(2,1)S(1)} collective-permute-done((bf16[32,8192]{1,0:T(8,128)(2,1)S(1)}, bf16[32,8192]{1,0:T(8,128)(2,1)S(1)}, u32[]{:S(2)}, u32[]{:S(2)}) %collective-permute-start.1) | collective-permute-done | bytes 524320 | tf_op jit(solution)/shard_map/while/body/eval_jaxpr/ppermute | solution.py:12
  331.6 6.3 %collective-permute-done.1 = bf16[32,8192]{1,0:T(8,128)(2,1)S(1)} collective-permute-done((bf16[32,8192]{1,0:T(8,128)(2,1)S(1)}, bf16[32,8192]{1,0:T(8,128)(2,1)S(1)}, u32[]{:S(2)}, u32[]{:S(2)}) %collective-permute-start.1) | collective-permute-done | bytes 524320 | tf_op jit(solution)/shard_map/while/body/eval_jaxpr/ppermute | solution.py:12
  341.6 2.2 bitcast_dynamic-update-slice_fusion.13
  350.1 6.3 %collective-permute-done.1 = bf16[32,8192]{1,0:T(8,128)(2,1)S(1)} collective-permute-done((bf16[32,8192]{1,0:T(8,128)(2,1)S(1)}, bf16[32,8192]{1,0:T(8,128)(2,1)S(1)}, u32[]{:S(2)}, u32[]{:S(2)}) %collective-permute-start.1) | collective-permute-done | bytes 524320 | tf_op jit(solution)/shard_map/while/body/eval_jaxpr/ppermute | solution.py:12
  356.5 12.8 %psum.7 = f32[4,2]{0,1:T(2,128)S(1)} all-reduce(f32[4,2]{0,1:T(2,128)S(1)} %copy.10), channel_id=1, replica_groups=mesh['section'=4,'dp'=8] {'section'}, use_global_device_ids=true, to_apply=%region_9.10 | all-reduce | flops 8 | bytes 64 | tf_op jit(solution)/shard_map/psum | solution.py:132
  369.5 2.6 fusion.28
  372.9 2.4 pad_maximum_fusion
  375.3 87.3 %reduce-scatter.2.cloned.1.call-done = bf16[1024,256]{0,1:T(8,128)(2,1)} async-done(((bf16[8192,256]{0,1:T(8,128)(2,1)}), bf16[1024,256]{0,1:T(8,128)(2,1)}) %reduce-scatter.2.cloned.1.call-update) | async-done | bytes 524304 | tf_op jit(solution)/shard_map/reduce_scatter | solution.py:144
  (286 shorter events, 143.1 us)
Async XLA Ops:
  7.2 55.0 %all-gather.3.cloned.1.call-start = ((), (), s32[]{:S(2)}) async-start(), calls=%async_computation.1 | async-start | bytes 2359296 | tf_op jit(solution)/shard_map/all_gather | solution.py:54
  7.9 104.3 %all-gather.5.cloned.1.call-start = ((), (), s32[]{:S(2)}) async-start(), calls=%async_computation.2 | async-start | bytes 2359296 | tf_op jit(solution)/shard_map/all_gather | solution.py:55
  8.6 453.9 %reduce-scatter.2.cloned.1.call-start = ((), (), s32[]{:S(2)}) async-start(), calls=%async_computation.3 | async-start | bytes 4718592 | tf_op jit(solution)/shard_map/reduce_scatter | solution.py:144
  112.2 3.1 copy-start
  121.6 3.5 collective-permute-start
  131.4 10.2 %collective-permute-start = (bf16[32,8192]{1,0:T(8,128)(2,1)S(1)}, bf16[32,8192]{1,0:T(8,128)(2,1)S(1)}, u32[]{:S(2)}, u32[]{:S(2)}) collective-permute-start(bf16[32,8192]{1,0:T(8,128)(2,1)S(1)} %fusion.73), channel_id=1, source_target_pairs={{0,8},{8,16},{16,24},{1,9},{9,17},{17,25},{2,10},{10,18},{18,26},{... | collective-permute-start | bytes 1572872 | tf_op jit(solution)/shard_map/while/body/eval_jaxpr/ppermute | solution.py:12
  147.9 10.5 %collective-permute-start = (bf16[32,8192]{1,0:T(8,128)(2,1)S(1)}, bf16[32,8192]{1,0:T(8,128)(2,1)S(1)}, u32[]{:S(2)}, u32[]{:S(2)}) collective-permute-start(bf16[32,8192]{1,0:T(8,128)(2,1)S(1)} %fusion.73), channel_id=1, source_target_pairs={{0,8},{8,16},{16,24},{1,9},{9,17},{17,25},{2,10},{10,18},{18,26},{... | collective-permute-start | bytes 1572872 | tf_op jit(solution)/shard_map/while/body/eval_jaxpr/ppermute | solution.py:12
  164.6 10.5 %collective-permute-start = (bf16[32,8192]{1,0:T(8,128)(2,1)S(1)}, bf16[32,8192]{1,0:T(8,128)(2,1)S(1)}, u32[]{:S(2)}, u32[]{:S(2)}) collective-permute-start(bf16[32,8192]{1,0:T(8,128)(2,1)S(1)} %fusion.73), channel_id=1, source_target_pairs={{0,8},{8,16},{16,24},{1,9},{9,17},{17,25},{2,10},{10,18},{18,26},{... | collective-permute-start | bytes 1572872 | tf_op jit(solution)/shard_map/while/body/eval_jaxpr/ppermute | solution.py:12
  181.4 10.5 %collective-permute-start = (bf16[32,8192]{1,0:T(8,128)(2,1)S(1)}, bf16[32,8192]{1,0:T(8,128)(2,1)S(1)}, u32[]{:S(2)}, u32[]{:S(2)}) collective-permute-start(bf16[32,8192]{1,0:T(8,128)(2,1)S(1)} %fusion.73), channel_id=1, source_target_pairs={{0,8},{8,16},{16,24},{1,9},{9,17},{17,25},{2,10},{10,18},{18,26},{... | collective-permute-start | bytes 1572872 | tf_op jit(solution)/shard_map/while/body/eval_jaxpr/ppermute | solution.py:12
  198.2 10.5 %collective-permute-start = (bf16[32,8192]{1,0:T(8,128)(2,1)S(1)}, bf16[32,8192]{1,0:T(8,128)(2,1)S(1)}, u32[]{:S(2)}, u32[]{:S(2)}) collective-permute-start(bf16[32,8192]{1,0:T(8,128)(2,1)S(1)} %fusion.73), channel_id=1, source_target_pairs={{0,8},{8,16},{16,24},{1,9},{9,17},{17,25},{2,10},{10,18},{18,26},{... | collective-permute-start | bytes 1572872 | tf_op jit(solution)/shard_map/while/body/eval_jaxpr/ppermute | solution.py:12
  214.9 10.5 %collective-permute-start = (bf16[32,8192]{1,0:T(8,128)(2,1)S(1)}, bf16[32,8192]{1,0:T(8,128)(2,1)S(1)}, u32[]{:S(2)}, u32[]{:S(2)}) collective-permute-start(bf16[32,8192]{1,0:T(8,128)(2,1)S(1)} %fusion.73), channel_id=1, source_target_pairs={{0,8},{8,16},{16,24},{1,9},{9,17},{17,25},{2,10},{10,18},{18,26},{... | collective-permute-start | bytes 1572872 | tf_op jit(solution)/shard_map/while/body/eval_jaxpr/ppermute | solution.py:12
  227.0 142.3 %copy-start.6 = (s32[4,2]{0,1:T(2,128)S(1)}, s32[4,2]{0,1:T(2,128)}, u32[]{:S(2)}) copy-start(s32[4,2]{0,1:T(2,128)} %param.17) | copy-start | bytes 100
  230.7 3.0 copy-start.3
  235.0 9.7 %collective-permute-start.1 = (bf16[32,8192]{1,0:T(8,128)(2,1)S(1)}, bf16[32,8192]{1,0:T(8,128)(2,1)S(1)}, u32[]{:S(2)}, u32[]{:S(2)}) collective-permute-start(bf16[32,8192]{1,0:T(8,128)(2,1)S(1)} %fusion.86), channel_id=1, source_target_pairs={{8,0},{16,8},{24,16},{9,1},{17,9},{25,17},{10,2},{18,10},{26,18},{... | collective-permute-start | bytes 1572872 | tf_op jit(solution)/shard_map/while/body/eval_jaxpr/ppermute | solution.py:12
  248.3 3.0 copy-start.3
  252.7 11.2 %collective-permute-start.1 = (bf16[32,8192]{1,0:T(8,128)(2,1)S(1)}, bf16[32,8192]{1,0:T(8,128)(2,1)S(1)}, u32[]{:S(2)}, u32[]{:S(2)}) collective-permute-start(bf16[32,8192]{1,0:T(8,128)(2,1)S(1)} %fusion.86), channel_id=1, source_target_pairs={{8,0},{16,8},{24,16},{9,1},{17,9},{25,17},{10,2},{18,10},{26,18},{... | collective-permute-start | bytes 1572872 | tf_op jit(solution)/shard_map/while/body/eval_jaxpr/ppermute | solution.py:12
  271.9 10.5 %collective-permute-start.1 = (bf16[32,8192]{1,0:T(8,128)(2,1)S(1)}, bf16[32,8192]{1,0:T(8,128)(2,1)S(1)}, u32[]{:S(2)}, u32[]{:S(2)}) collective-permute-start(bf16[32,8192]{1,0:T(8,128)(2,1)S(1)} %fusion.86), channel_id=1, source_target_pairs={{8,0},{16,8},{24,16},{9,1},{17,9},{25,17},{10,2},{18,10},{26,18},{... | collective-permute-start | bytes 1572872 | tf_op jit(solution)/shard_map/while/body/eval_jaxpr/ppermute | solution.py:12
  290.4 10.5 %collective-permute-start.1 = (bf16[32,8192]{1,0:T(8,128)(2,1)S(1)}, bf16[32,8192]{1,0:T(8,128)(2,1)S(1)}, u32[]{:S(2)}, u32[]{:S(2)}) collective-permute-start(bf16[32,8192]{1,0:T(8,128)(2,1)S(1)} %fusion.86), channel_id=1, source_target_pairs={{8,0},{16,8},{24,16},{9,1},{17,9},{25,17},{10,2},{18,10},{26,18},{... | collective-permute-start | bytes 1572872 | tf_op jit(solution)/shard_map/while/body/eval_jaxpr/ppermute | solution.py:12
  304.6 3.1 copy-start.3
  308.9 10.5 %collective-permute-start.1 = (bf16[32,8192]{1,0:T(8,128)(2,1)S(1)}, bf16[32,8192]{1,0:T(8,128)(2,1)S(1)}, u32[]{:S(2)}, u32[]{:S(2)}) collective-permute-start(bf16[32,8192]{1,0:T(8,128)(2,1)S(1)} %fusion.86), channel_id=1, source_target_pairs={{8,0},{16,8},{24,16},{9,1},{17,9},{25,17},{10,2},{18,10},{26,18},{... | collective-permute-start | bytes 1572872 | tf_op jit(solution)/shard_map/while/body/eval_jaxpr/ppermute | solution.py:12
  323.1 3.0 copy-start.3
  327.4 10.5 %collective-permute-start.1 = (bf16[32,8192]{1,0:T(8,128)(2,1)S(1)}, bf16[32,8192]{1,0:T(8,128)(2,1)S(1)}, u32[]{:S(2)}, u32[]{:S(2)}) collective-permute-start(bf16[32,8192]{1,0:T(8,128)(2,1)S(1)} %fusion.86), channel_id=1, source_target_pairs={{8,0},{16,8},{24,16},{9,1},{17,9},{25,17},{10,2},{18,10},{26,18},{... | collective-permute-start | bytes 1572872 | tf_op jit(solution)/shard_map/while/body/eval_jaxpr/ppermute | solution.py:12
  341.6 3.1 copy-start.3
  345.9 10.5 %collective-permute-start.1 = (bf16[32,8192]{1,0:T(8,128)(2,1)S(1)}, bf16[32,8192]{1,0:T(8,128)(2,1)S(1)}, u32[]{:S(2)}, u32[]{:S(2)}) collective-permute-start(bf16[32,8192]{1,0:T(8,128)(2,1)S(1)} %fusion.86), channel_id=1, source_target_pairs={{8,0},{16,8},{24,16},{9,1},{17,9},{25,17},{10,2},{18,10},{26,18},{... | collective-permute-start | bytes 1572872 | tf_op jit(solution)/shard_map/while/body/eval_jaxpr/ppermute | solution.py:12
  (18 other events, 38.1 us)
Sparse Core Ops, SparseCore 0:
  10.1 52.0 all-gather.2
  64.4 47.7 all-gather.4
  375.4 87.0 reduce-scatter.1
where the time goes:
time: 475 us; the launch traced here: 472 us
  waiting for transfers between devices  203 us (43%)
  starting transfers between devices  60.1 us (13%)
  other arithmetic  55.6 us (12%)
  local copies, waits for them, and re-layouts  48.7 us (10%)
  blocking collectives  45.3 us (10%)
  matrix products  36.2 us (8%)
  between operations  13.9 us (3%)
  loops' own time  9.39 us (2%)
    reduce_scatter x1, waiting for transfers between devices, shards(): lax.psum_scatter(jnp.concatenate([contract_first(normed_rows, weighted_er...  87.3 us
    ppermute x14, starting transfers between devices, from_behind(): return lax.ppermute(block, axis, route)  60 us
    all_gather x1, waiting for transfers between devices, shards(): lax.all_gather(adapter_out, 'dp', axis=2, tiled=True)  50 us
    ppermute x14, waiting for transfers between devices, from_behind(): return lax.ppermute(block, axis, route)  44 us
    dynamic_update_slice x21, other arithmetic, place(): lax.dynamic_update_index_in_dim(store, jnp.where(active, value, old), ind...  37.4 us
    all_gather x1, blocking collectives, shards(): lax.all_gather(norm_gain, 'dp', axis=1, tiled=True)  32.4 us
    dot_general x42, matrix products, contract_last(): lax.dot_general(left, right, (((1,), (1,)), ((), ())), preferred_element_...  26.6 us
    dynamic_slice x35, local copies, waits for them, and re-layouts, place(): old = lax.dynamic_index_in_dim(store, index, 0, keepdims=False)  22.8 us
  transfers between devices with their start and end apart: 17, of which 10 were waited for; matrix products, arithmetic and copies ran while one was open for 8% of the time, Pallas kernels for 0%

commit v1 on v0

v1 whole, which is shorter than its diff:
```python
import functools
import math

import jax
import jax.numpy as jnp
from jax import lax
from jax.experimental import pallas as pl
from jax.experimental.pallas import tpu as pltpu
from jax.sharding import PartitionSpec as P

F32 = jnp.float32
BF16 = jnp.bfloat16
VMEM = pl.BlockSpec(memory_space=pltpu.VMEM)
SMEM = pl.BlockSpec(memory_space=pltpu.SMEM)
FAR = pl.BlockSpec(memory_space=pltpu.HBM)
ANY = pl.BlockSpec(memory_space=pl.ANY)
LIMIT = 16 * 1024 * 1024
LANES = 128
PAD = 16


def dot(left, right):
    return jnp.dot(left.astype(BF16), right.astype(BF16), preferred_element_type=F32)


def dot_last(left, right):
    return lax.dot_general(
        left.astype(BF16), right.astype(BF16), (((1,), (1,)), ((), ())), preferred_element_type=F32
    )


def dot_first(left, right):
    return lax.dot_general(
        left.astype(BF16), right.astype(BF16), (((0,), (0,)), ((), ())), preferred_element_type=F32
    )


def swap(block, axis, bit):
    size = lax.axis_size(axis)
    return lax.ppermute(block, axis, [(i, i ^ bit) for i in range(size)])


def exchange(blocks):
    return lax.all_to_all(blocks, "dp", 0, 0, tiled=True)


def out_in_vmem(shape, dtype):
    return pltpu.VMEM(shape, dtype)


def call(body, outs, specs, pinned=(), limit=LIMIT, **options):
    return pl.pallas_call(
        body,
        out_shape=[
            out_in_vmem(*out) if i in pinned else jax.ShapeDtypeStruct(*out)
            for i, out in enumerate(outs)
        ],
        in_specs=specs,
        out_specs=options.pop("out_specs", [VMEM] * len(outs)),
        compiler_params=pltpu.CompilerParams(vmem_limit_bytes=limit),
        **options,
    )


def in_hbm(*arrays):
    return [pltpu.with_memory_space_constraint(array, pltpu.HBM) for array in arrays]


def in_vmem(*arrays):
    return [pltpu.with_memory_space_constraint(array, pltpu.VMEM) for array in arrays]


def down_of(packs, layer, slab):
    return packs[layer, slab : 2 * slab, :]


def unchunk(block):
    rank = block.shape[1]
    return jnp.concatenate(
        [block[c * rank : (c + 1) * rank] for c in range(block.shape[0] // rank)], 1
    )


def up_of(packs, layer, slab):
    return unchunk(packs[layer, :slab, :])


def gain_of(packs, layer, slab):
    rank = packs.shape[2]
    rows = packs[layer, 2 * slab : 2 * slab + PAD, :].astype(F32)
    return jnp.concatenate([rows[c : c + 1, :] for c in range(slab // rank)], 1)


def first_micro(copies, share):
    return (lax.axis_index("section") // copies) * share


def split_kernel(copies, h_ref, c_ref, out_ref, sems):
    parts, _, own, slab = out_ref.shape
    rows = h_ref.shape[1]
    share = own // rows
    first = first_micro(copies, share)
    copies = []
    for i, whole in enumerate((h_ref, c_ref)):
        for n in range(parts):
            for m in range(share):
                copy = pltpu.make_async_copy(
                    whole.at[first + m, :, pl.ds(n * slab, slab)],
                    out_ref.at[n, i, pl.ds(m * rows, rows), :],
                    sems.at[i, n, m],
                )
                copy.start()
                copies.append(copy)
    for copy in copies:
        copy.wait()


def pack_kernel(down_ref, up_ref, gain_ref, up_out, down_out):
    slab, rank = down_ref.shape[1:]
    gain = gain_ref[...].astype(F32)
    parts = [gain[:, c * rank : (c + 1) * rank] for c in range(slab // rank)]
    for c, row in enumerate(parts):
        here = slice(c * rank, (c + 1) * rank)
        column = jnp.broadcast_to(row, (rank, rank)).T
        up_out[here, :] = up_ref[0, :, here]
        down_out[here, :] = (down_ref[0, here, :].astype(F32) * column).astype(BF16)
    spare = [jnp.zeros((PAD - len(parts), rank), F32)]
    down_out[slab:, :] = jnp.concatenate(parts + spare, 0).astype(BF16)


def products_kernel(down_ref, *refs):
    *pieces, gram_ref, ups_ref, sems = refs
    sections, slab, _ = ups_ref.shape
    rank = down_ref.shape[1]
    section = lax.axis_index("section")
    copies = [
        pltpu.make_async_copy(piece, ups_ref.at[section ^ offset], sems.at[i])
        for i, (piece, offset) in enumerate(zip(pieces, gathered_offsets(sections)))
    ]
    for copy in copies:
        copy.start()
    for copy in copies:
        copy.wait()
    own = unchunk(ups_ref[section])
    down = down_ref[:slab, :]
    for j in range(sections - 1):
        up = unchunk(ups_ref[j])
        value = jnp.where(j < section, dot(up, down), dot_last(own, up))
        gram_ref[j * rank : (j + 1) * rank, :] = value.astype(BF16)


def packs_kernel(*refs):
    *pieces, packs_ref, token_ref, sems = refs
    section = lax.axis_index("section")
    sections = packs_ref.shape[0]
    copies = []
    for i, offset in enumerate(gathered_offsets(sections)):
        begin = 0
        for j in range(2):
            piece = pieces[j * sections + i]
            target = packs_ref.at[section ^ offset, pl.ds(begin, piece.shape[0]), :]
            copies.append(pltpu.make_async_copy(piece, target, sems.at[j, i]))
            begin += piece.shape[0]
    for copy in copies:
        copy.start()
    token_ref[...] = jnp.zeros_like(token_ref)
    for copy in copies:
        copy.wait()


def gathered_offsets(sections, lowest=1):
    offsets = [0]
    bit = sections // 2
    while bit >= lowest:
        offsets = offsets + [offset ^ bit for offset in offsets]
        bit //= 2
    return offsets


def gather(block, lowest=1):
    pieces = gather_far(block, lowest)
    return pieces + [swap(piece, "section", lowest) for piece in pieces]


def gather_far(block, lowest):
    pieces = [block]
    bit = lax.axis_size("section") // 2
    while bit > lowest:
        pieces = pieces + [swap(piece, "section", bit) for piece in pieces]
        bit //= 2
    return pieces


def tie_kernel(block_ref, _, out_ref):
    del block_ref, out_ref


def add_tie_kernel(block_ref, sent_ref, came_ref, out_ref, sum_ref):
    del block_ref, out_ref
    sum_ref[...] = (sent_ref[...].astype(F32) + came_ref[...].astype(F32)).astype(BF16)


def add_tie(block, sent, came):
    return call(
        add_tie_kernel,
        [(block.shape, block.dtype), (sent.shape, sent.dtype)],
        [ANY, VMEM, VMEM],
        out_specs=[ANY, VMEM],
        input_output_aliases={0: 0},
    )(block, sent, came)


def tie(block, after):
    return call(
        tie_kernel,
        [(block.shape, block.dtype)],
        [ANY] * 2,
        out_specs=[ANY],
        input_output_aliases={0: 0},
    )(block, after)[0]


def notes_kernel(
    copies, slices_ref, h_ref, users_ref, included_ref, _, one_ref, two_ref, notes_ref, h_held, sem
):
    share, rows, _ = h_held.shape
    users = included_ref.shape[1]
    first = first_micro(copies, share)
    copy = pltpu.make_async_copy(h_ref.at[pl.ds(first, share)], h_held, sem)
    copy.start()
    cut = one_ref.shape[0]
    one_ref[...] = slices_ref[:cut]
    two_ref[...] = slices_ref[cut:]
    copy.wait()
    lane = lax.broadcasted_iota(jnp.int32, (rows, LANES), 1)
    diagonal = lax.broadcasted_iota(jnp.int32, (rows, rows), 0) == lax.broadcasted_iota(
        jnp.int32, (rows, rows), 1
    )
    for m in range(share):
        ids = users_ref[pl.ds(first + m, 1), :] - lax.axis_index("dp") * users
        column = jnp.sum(jnp.where(diagonal, ids, 0), -1, keepdims=True)
        wanted = included_ref[pl.ds(first + m, 1), :]
        chosen = jnp.zeros((rows, 1), jnp.int32)
        for u in range(users):
            chosen = chosen + jnp.where(column == u, wanted[:, u : u + 1], 0)
        wide = h_held[m].astype(F32)
        square = jnp.sum(wide * wide, -1, keepdims=True)
        notes = jnp.where(lane == 0, column.astype(F32), 0.0)
        notes = jnp.where(lane == 1, chosen.astype(F32), notes)
        notes_ref[m * rows : (m + 1) * rows, :] = jnp.where(lane == 2, square, notes)


def add_kernel(one_ref, two_ref, _, out_ref):
    out_ref[...] = (one_ref[...].astype(F32) + two_ref[...].astype(F32)).astype(BF16)


def project_kernel(slices_ref, packs_ref, _, out_ref):
    parts, _, own, slab = slices_ref.shape
    sections, _, rank = packs_ref.shape
    slice_h = slices_ref[:, 0].reshape(parts * own, slab)
    slice_c = slices_ref[:, 1].reshape(parts * own, slab)

    def put(value, index):
        here = slice(index * own, (index + 1) * own)
        out_ref[:, here, :] = value.astype(BF16).reshape(parts, own, rank)

    for l in range(sections):
        put(dot(slice_h, down_of(packs_ref, l, slab)), l)
    for l in range(sections):
        up = up_of(packs_ref, l, slab)
        put(dot_last(slice_c, up), 2 * sections - 1 + l)
        if l < sections - 1:
            put(dot_last(slice_h, up), sections + l)


def solve_kernel(width, notes_far, payload_ref, *refs):
    *pieces, out_ref, gram_ref, notes_ref, sems = refs
    pieces = pieces[3:]
    own = notes_ref.shape[0]
    parts, size, rank = out_ref.shape
    layers = (size // own - 1) // 2
    each = gram_ref.shape[0] // layers
    section = lax.axis_index("section")
    copies = [pltpu.make_async_copy(notes_far, notes_ref, sems.at[layers])]
    for i, (piece, offset) in enumerate(zip(pieces, gathered_offsets(layers))):
        begin = pl.multiple_of((section ^ offset) * each, each)
        copies.append(pltpu.make_async_copy(piece, gram_ref.at[pl.ds(begin, each), :], sems.at[i]))
    for copy in copies:
        copy.start()
    def column(index):
        return jnp.sum(payload_ref[:, index * own : (index + 1) * own, :].astype(F32), 0)

    def put(value, index):
        here = slice(index * own, (index + 1) * own)
        out_ref[:, here, :] = jnp.broadcast_to(value[None], (parts, own, rank))

    p = [column(i) for i in range(layers)]
    through = [column(layers + i) for i in range(layers - 1)]
    e = [column(2 * layers - 1 + i) for i in range(layers)]
    for copy in copies:
        copy.wait()
    gram = [
        [gram_ref[s * each + j * rank : s * each + (j + 1) * rank, :] for j in range(layers - 1)]
        for s in range(layers)
    ]
    square = notes_ref[:, 2:3]
    seen, low, exact, scale = [], [], [], []
    for l in range(layers):
        seen.append(list(through))
        scale.append(lax.rsqrt(jnp.maximum(square, 0.0) / width + 1e-05))
        exact.append(scale[l] * p[l])
        low.append(exact[l].astype(BF16))
        if l == layers - 1:
            break
        for k in range(l + 1, layers):
            p[k] = p[k] + dot(low[l], gram[k][l])
        before = through[l]
        for k in range(layers - 1):
            if k >= l:
                through[k] = through[k] + dot(low[l], gram[l][k])
            else:
                through[k] = through[k] + dot_last(low[l], gram[k][l])
        square = square + jnp.sum(low[l].astype(F32) * (before + through[l]), -1, keepdims=True)
    lane = lax.broadcasted_iota(jnp.int32, (own, rank), 1)
    extra = jnp.where(lane == 2 * layers, notes_ref[:, :1], 0.0)
    extra = jnp.where(lane == 2 * layers + 1, notes_ref[:, 1:2], extra)
    for l in range(layers - 1, -1, -1):
        err = e[l]
        mean = jnp.sum(err * exact[l], -1, keepdims=True) / width
        alpha = scale[l] * scale[l] * mean
        scaled = (scale[l] * err).astype(BF16)
        for k in range(l):
            e[k] = e[k] + dot_last(scaled, gram[l][k]) - alpha * seen[l][k]
        put(low[l], l)
        put(scaled, layers + l)
        coarse = alpha.astype(BF16).astype(F32)
        extra = jnp.where(lane == l, coarse, extra)
        extra = jnp.where(lane == layers + l, alpha - coarse, extra)
    put(extra.astype(BF16), 2 * layers)


def spread(extra, columns):
    rank = extra.shape[1]
    row = lax.broadcasted_iota(jnp.int32, (rank, rank), 0)
    picks = []
    for column in columns:
        pick = row == column[0]
        for other in column[1:]:
            pick = pick | (row == other)
        picks.append(jnp.where(pick, 1.0, 0.0).astype(BF16))
    wide = dot(extra, jnp.concatenate(picks, 1))
    return [wide[:, i * rank : (i + 1) * rank] for i in range(len(columns))]


def tiled(block, width):
    return jnp.concatenate([block] * (width // block.shape[1]), 1)


def place_of(counts, dimension, lanes):
    rows = math.prod(counts)
    return lax.broadcasted_iota(jnp.int32, counts + (lanes,), dimension).reshape(rows, lanes)


def user_lanes(ids, counts, users, lanes, m):
    lane = lax.broadcasted_iota(jnp.int32, (ids.shape[0], lanes), 1)
    user = tiled(ids, lanes).astype(jnp.int32) + place_of(counts, 0, lanes) * users
    mine = lane == user
    return mine if counts[1] == 1 else mine & (place_of(counts, 1, lanes) == m)


def state_rows(ref, index, own):
    parts, _, rank = ref.shape
    return ref[:, index * own : (index + 1) * own, :].reshape(parts * own, rank)


def streams_kernel(
    rows, users, slices_ref, packs_ref, states_ref, ghosts_ref, passed_ref, streams_ref, sem
):
    parts, _, own, slab = slices_ref.shape
    layers, _, rank = packs_ref.shape
    everyone = parts * own
    counts = (parts, own // rows, rows)
    passing = pltpu.make_async_copy(states_ref, passed_ref, sem)
    passing.start()

    def state(index):
        return state_rows(states_ref, index, own)

    extra = state(2 * layers)
    columns = [(2 * layers,)] + [(l, layers + l) for l in range(1, layers)]
    ids, *alphas = spread(extra, columns)
    step = rows
    while step < 256 and everyone % (2 * step) == 0:
        step *= 2
    spans = [slice(at, at + step) for at in range(0, everyone, step)]
    pairs = [jnp.zeros((step, step), F32) for _ in spans]
    stream = slices_ref[:, 0].reshape(everyone, slab)
    wide = stream.astype(F32)
    for l in range(layers):
        streams_ref[l] = stream
        low, scaled = state(l), state(layers + l)
        normed = (wide * gain_of(packs_ref, l, slab)).astype(BF16)
        for at, here in enumerate(spans):
            pairs[at] += dot_last(normed[here], normed[here]) * dot_last(scaled[here], scaled[here])
        if l < layers - 1:
            wide = wide + dot(low, up_of(packs_ref, l, slab))
            stream = wide.astype(BF16)
    delta = slices_ref[:, 1].reshape(everyone, slab)
    wide = delta.astype(F32)
    for l in range(layers - 1, -1, -1):
        low = state(l)
        for at, here in enumerate(spans):
            pairs[at] += dot_last(low[here], low[here]) * dot_last(delta[here], delta[here])
        if l > 0:
            wide = wide + dot_last(state(layers + l), down_of(packs_ref, l, slab))
            wide = wide - tiled(alphas[l - 1], slab) * streams_ref[l].astype(F32)
            delta = wide.astype(BF16)
    block = place_of((everyone // rows, rows), 0, rank).astype(F32)
    numbers = ids + block * users
    rowsums = []
    for at, here in enumerate(spans):
        number = numbers[here]
        other = jnp.transpose(number)[:1, :]
        own_number = tiled(number, step) if step >= rank else number[:, :step]
        rowsums.append(
            jnp.sum(jnp.where(own_number == other, pairs[at], 0.0), -1, keepdims=True)
        )
    rowsum = jnp.concatenate(rowsums, 0)
    copies, share, lanes = ghosts_ref.shape
    for m in range(share):
        mine = user_lanes(ids, counts, users, lanes, m)
        total = jnp.sum(jnp.where(mine, rowsum, 0.0), 0, keepdims=True)
        ghosts_ref[:, m : m + 1, :] = jnp.broadcast_to(total[None], (copies, 1, lanes))
    passing.wait()


def grads_kernel(rows, users, bound, copies, packs_ref, *refs):
    count = (len(refs) - 12) // 3
    one_pieces, two_pieces, state_pieces = (refs[i * count : (i + 1) * count] for i in range(3))
    (
        ghosts_ref,
        included_ref,
        in_ref,
        out_ref,
        weights_ref,
        h_held,
        c_held,
        state_held,
        clips_ref,
        h_sum,
        c_sum,
        sems,
    ) = refs[3 * count :]
    layers, _, rank = packs_ref.shape
    _, parts, own, slab = h_held.shape
    cut = one_pieces[0].shape[0]
    everyone = parts * own
    share, lanes = ghosts_ref.shape[2:]
    section = lax.axis_index("section")
    offsets = gathered_offsets(layers, copies)

    def moves(at, entry):
        one, two = pl.ds(0, cut), pl.ds(cut, parts - cut)
        return [
            pltpu.make_async_copy(state_pieces[entry], state_held.at[at], sems.at[at, 0]),
            pltpu.make_async_copy(one_pieces[entry].at[:, 0], h_held.at[at, one], sems.at[at, 1]),
            pltpu.make_async_copy(two_pieces[entry].at[:, 0], h_held.at[at, two], sems.at[at, 2]),
            pltpu.make_async_copy(one_pieces[entry].at[:, 1], c_held.at[at, one], sems.at[at, 3]),
            pltpu.make_async_copy(two_pieces[entry].at[:, 1], c_held.at[at, two], sems.at[at, 4]),
        ]

    for entry in range(count):
        for move in moves(entry, entry):
            move.start()
    h_sum[...] = jnp.zeros_like(h_sum)
    c_sum[...] = jnp.zeros_like(c_sum)
    columns = [(2 * layers,), (2 * layers + 1,)]
    for k in range(1, layers):
        taken = [jnp.where(l > section, l, -1) for l in range(k, layers)]
        columns.append(taken + [jnp.where(l >= 0, layers + l, -1) for l in taken])
    group = max(1, min(count, 512 // everyone))

    @pl.loop(0, count // group)
    def _(step):
        begin = step * group
        scaled, low, rest = [], [], [[] for _ in range(layers - 1)]
        for i in range(group):
            at = begin + i
            for move in moves(at, 0):
                move.wait()
            offset = sum(jnp.where(at == n, value, 0) for n, value in enumerate(offsets))
            there = section ^ offset
            totals = sum(ghosts_ref[there, n] for n in range(parts))
            clips = bound / jnp.maximum(jnp.sqrt(totals), bound)
            clips_ref[pl.ds((there // copies) * share, share), :] = clips
            state_ref = state_held.at[at]
            ids, included, *alphas = spread(state_rows(state_ref, 2 * layers, own), columns)
            weight = jnp.zeros((everyone, 1), F32)
            for m in range(share):
                mine = user_lanes(ids, (parts, share, rows), users, lanes, m)
                weight += jnp.sum(jnp.where(mine, clips[m : m + 1, :], 0.0), -1, keepdims=True)
            weight = weight * included

            def weighted(index):
                first = pl.multiple_of(index * own, own)
                block = state_ref[:, pl.ds(first, own), :].reshape(everyone, rank)
                return weight * block.astype(F32)

            scaled.append(weighted(layers + section).astype(BF16))
            low.append(weighted(section))
            for k in range(layers - 1):
                rest[k].append((alphas[k] * low[i]).astype(BF16))
        here = pl.ds(begin, group)

        def everything(ref, *index):
            return ref[(here,) + index].reshape(group * everyone, -1)

        def known(index):
            return everything(state_held, slice(None), slice(index * own, (index + 1) * own))

        scaled = jnp.concatenate(scaled, 0)
        low = jnp.concatenate(low, 0).astype(BF16)
        for k in range(layers - 1):
            sides = jnp.concatenate([scaled, jnp.concatenate(rest[k], 0)], 1)
            if k == 0:
                h_sum[:, :slab] += dot_first(sides, everything(h_held))
            h_sum[:, slab + k * rank : slab + (k + 1) * rank] += dot_first(sides, known(k))
        c_sum[:, :slab] += dot_first(low, everything(c_held))
        errs = jnp.concatenate([known(layers + k) for k in range(layers)], 1)
        c_sum[:, slab:] += dot_first(low, errs)

    left, right = h_sum[:rank, :slab], c_sum[:, :slab] - h_sum[rank:, :slab]
    for k in range(layers):
        beside = slice(slab + k * rank, slab + (k + 1) * rank)
        later = (k > section).astype(F32)
        right += dot_last(later * c_sum[:, beside], down_of(packs_ref, k, slab))
        if k < layers - 1:
            up = up_of(packs_ref, k, slab)
            earlier = (k < section).astype(F32)
            left += dot(earlier * h_sum[:rank, beside], up)
            right -= dot(h_sum[rank:, beside], up)
    out_ref[0] = right
    left = left * gain_of(packs_ref, section, slab)
    for c in range(slab // rank):
        part = slice(c * rank, (c + 1) * rank)
        in_ref[0, part, :] = left[:, part].T
    users_here, micro = included_ref.shape
    mine = lax.broadcasted_iota(jnp.int32, (micro, lanes), 1) - lax.axis_index("dp") * users
    diagonal = lax.broadcasted_iota(jnp.int32, (micro, micro), 0) == lax.broadcasted_iota(
        jnp.int32, (micro, micro), 1
    )
    for u in range(users_here):
        column = jnp.sum(jnp.where(mine == u, clips_ref[...], 0.0), -1, keepdims=True)
        row = jnp.sum(jnp.where(diagonal, column, 0.0), 0, keepdims=True)
        weights_ref[u : u + 1, :] = included_ref[u : u + 1, :].astype(F32) * row


def sum_parts(value, token):
    size = lax.axis_size("dp")
    bits = [1 << i for i in range(1, size.bit_length() - 1)]
    for bit in bits:
        came = swap(value, "dp", bit)
        if bit != bits[-1]:
            value = (value.astype(F32) + came.astype(F32)).astype(BF16)
        else:
            (value,) = call(add_kernel, [(value.shape, BF16)], [VMEM] * 3)(value, came, token)
    return value, swap(value, "dp", 1)


def shards(hidden_in, cotangent, adapter_in, adapter_out, norm_gain, user_of_row, included):
    sections = lax.axis_size("section")
    section = lax.axis_index("section")
    parts = lax.axis_size("dp")
    dp_index = lax.axis_index("dp")
    micro, rows, width = hidden_in.shape
    rank = adapter_in.shape[2]
    users = included.shape[1]
    layers = sections
    slab = width // parts
    share = max(1, micro // sections)
    copies = max(1, sections // micro)
    own = share * rows
    everyone = parts * own

    up, down = call(
        pack_kernel, [((slab, rank), BF16), ((slab + PAD, rank), BF16)], [VMEM] * 3
    )(*in_hbm(adapter_in, adapter_out, norm_gain))
    ups = gather(up)
    downs = gather(down)
    (blocks,) = call(
        functools.partial(split_kernel, copies),
        [((parts, 2, own, slab), BF16)],
        [FAR, FAR],
        scratch_shapes=[pltpu.SemaphoreType.DMA((2, parts, share))],
    )(*in_hbm(hidden_in, cotangent))
    slices = exchange(blocks)

    each = (layers - 1) * rank
    (gram,) = call(
        products_kernel,
        [((each, rank), BF16)],
        [VMEM, FAR] + [ANY] * (sections - 1),
        scratch_shapes=[
            pltpu.VMEM((sections, slab, rank), BF16),
            pltpu.SemaphoreType.DMA((sections,)),
        ],
    )(down, *in_hbm(up), *ups[1:])
    packs, token = call(
        packs_kernel,
        [((sections, 2 * slab + PAD, rank), BF16), ((8, LANES), F32)],
        [FAR] * (2 * sections),
        pinned=(0,),
        scratch_shapes=[pltpu.SemaphoreType.DMA((2, sections))],
    )(*in_hbm(*ups, *downs))
    sent, came = sum_parts(gram, token)

    (payload,) = call(
        project_kernel,
        [((parts, (3 * layers - 1) * own, rank), BF16)],
        [VMEM, VMEM, ANY],
    )(slices, *in_vmem(packs), sent)
    payload, gram = add_tie(payload, sent, came)
    payload = exchange(payload)
    grams = gather(gram)
    cut = max(1, parts * 2 // 8)
    one, two, notes = call(
        functools.partial(notes_kernel, copies),
        [
            ((cut, 2, own, slab), BF16),
            ((parts - cut, 2, own, slab), BF16),
            ((own, LANES), F32),
        ],
        [VMEM, FAR, VMEM, VMEM, ANY],
        scratch_shapes=[pltpu.VMEM((share, rows, width), BF16), pltpu.SemaphoreType.DMA],
    )(slices, *in_hbm(hidden_in), user_of_row, included, grams[1])
    ones = gather_far(one, copies)
    twos = gather_far(two, copies)
    ones_own, twos_own = swap(one, "section", copies), swap(two, "section", copies)
    count = 2 * len(ones)

    (state,) = call(
        functools.partial(solve_kernel, width),
        [((parts, (2 * layers + 1) * own, rank), BF16)],
        [FAR, VMEM] + [FAR] * (3 + len(grams)),
        scratch_shapes=[
            pltpu.VMEM((layers * each, rank), BF16),
            pltpu.VMEM((own, LANES), F32),
            pltpu.SemaphoreType.DMA((layers + 1,)),
        ],
    )(*in_hbm(notes), payload, *in_hbm(ones[1], ones_own, twos_own, *grams))
    states = exchange(state)

    lanes = -(-users * parts // LANES) * LANES
    ghosts, mine = call(
        functools.partial(streams_kernel, rows, users),
        [((sections * parts, share, lanes), F32), (states.shape, BF16)],
        [VMEM] * 3,
        out_specs=[VMEM, FAR],
        scratch_shapes=[
            pltpu.VMEM((layers, everyone, slab), BF16),
            pltpu.SemaphoreType.DMA,
        ],
    )(slices, *in_vmem(packs), states)
    states_far = gather_far(states, copies)
    ghosts = lax.all_to_all(ghosts, ("section", "dp"), 0, 0, tiled=True)
    ones = ones[:1] + [tie(piece, ghosts) for piece in ones[1:]]
    twos = twos[:1] + [tie(piece, ghosts) for piece in twos[1:]]
    ones = ones + [ones_own] + [swap(piece, "section", copies) for piece in ones[1:]]
    twos = twos + [twos_own] + [swap(piece, "section", copies) for piece in twos[1:]]
    states = [tie(mine, ghosts)] + [tie(piece, ghosts) for piece in states_far[1:]]
    states = states + [swap(piece, "section", copies) for piece in states]
    ghosts = ghosts.reshape(sections, parts, share, lanes)
    bound = 0.8 * math.sqrt(sections * (rows // users) * width * width)

    grad_in, grad_out, weights = call(
        functools.partial(grads_kernel, rows, users, bound, copies),
        [((1, slab, rank), F32), ((1, rank, slab), F32), ((users, micro), F32)],
        [VMEM] + [FAR] * (2 * count + 1) + [ANY] * (count - 1) + [VMEM] * 2,
        limit=LIMIT + 3 * count * (states[0].size + slices.size),
        scratch_shapes=[
            pltpu.VMEM((count, parts, own, slab), BF16),
            pltpu.VMEM((count, parts, own, slab), BF16),
            pltpu.VMEM((count,) + states[0].shape, BF16),
            pltpu.VMEM((micro, lanes), F32),
            pltpu.VMEM((2 * rank, slab + (layers - 1) * rank), F32),
            pltpu.VMEM((rank, slab + layers * rank), F32),
            pltpu.SemaphoreType.DMA((count, 5)),
        ],
    )(
        *in_vmem(packs),
        *in_hbm(*ones, *twos, states[0]),
        *states[1:],
        ghosts,
        included.T,
    )
    return (grad_in, grad_out, weights.T)


def solution(mesh):
    placed = (
        P(None, "dp", None),
        P(None, "dp", None),
        P("section", "dp", None),
        P("section", None, "dp"),
        P("section", "dp"),
        P(None, "dp"),
        P(None, "dp"),
    )
    return jax.shard_map(
        shards,
        mesh=mesh,
        in_specs=placed,
        out_specs=(P("section", "dp", None), P("section", None, "dp"), P(None, "dp")),
        check_vma=False,
    )
```

time: 475 us -> 120 us (0.25)
  waiting for transfers between devices: 203 us -> 52.1 us
  other arithmetic: 55.6 us -> 0.03 us
  blocking collectives: 45.3 us -> 0 us
  local copies, waits for them, and re-layouts: 48.7 us -> 3.83 us
  matrix products: 36.2 us -> 0 us
  Pallas kernels: 0 us -> 24.7 us
  starting transfers between devices: 60.1 us -> 37.7 us
  between operations: 13.9 us -> 0.94 us
  loops' own time: 9.39 us -> 0 us
    reduce_scatter x1 -> x0, waiting for transfers between devices: 87.3 us -> none  [shards(): lax.psum_scatter(jnp.concatenate([contract_first(normed_rows, weighted_er...]
    all_gather x2 -> x0, waiting for transfers between devices: 70.3 us -> none  [the longest x1 50 us: shards(): lax.all_gather(adapter_out, 'dp', axis=2, tiled=True)]
    ppermute x14 -> x21, starting transfers between devices: 60 us -> 19.2 us  [swap(): return lax.ppermute(block, axis, [(i, i ^ bit) for i in range(size)])]
    dynamic_update_slice x21 -> x0, other arithmetic: 37.4 us -> none  [place(): lax.dynamic_update_index_in_dim(store, jnp.where(active, value, old), ind...]
    dot_general x58 -> x0, matrix products: 36.2 us -> none  [the longest x42 26.6 us: contract_last(): lax.dot_general(left, right, (((1,), (1,)), ((), ())), preferred_element_...]
    all_gather x1 -> x0, blocking collectives: 32.4 us -> none  [shards(): lax.all_gather(norm_gain, 'dp', axis=1, tiled=True)]
    dynamic_slice x49 -> x0, local copies, waits for them, and re-layouts: 30.8 us -> none  [the longest x35 22.8 us: place(): old = lax.dynamic_index_in_dim(store, index, 0, keepdims=False)]
    pallas_call x0 -> x15, Pallas kernels: none -> 24.7 us  [the longest x1 6.4 us: shards(): call(functools.partial(grads_kernel, rows, users, bound, copies), [((1, s...]
  transfers between devices with their start and end apart: 17 -> 25, of which waited for: 10 -> 14; matrix products, arithmetic and copies ran while one was open for 8% -> 0% of each run, Pallas kernels for 0% -> 10%
where the time goes in v1:
time: 120 us; the launch traced here: 119 us
  waiting for transfers between devices  52.1 us (43%)
  starting transfers between devices  37.7 us (31%)
  Pallas kernels  24.7 us (21%)
  local copies, waits for them, and re-layouts  3.83 us (3%)
    ppermute x21, waiting for transfers between devices, swap(): return lax.ppermute(block, axis, [(i, i ^ bit) for i in range(size)])  28.6 us
    ppermute x21, starting transfers between devices, swap(): return lax.ppermute(block, axis, [(i, i ^ bit) for i in range(size)])  19.2 us
    all_to_all x3, waiting for transfers between devices, exchange(): return lax.all_to_all(blocks, 'dp', 0, 0, tiled=True)  16.2 us
    all_to_all x3, starting transfers between devices, exchange(): return lax.all_to_all(blocks, 'dp', 0, 0, tiled=True)  15.8 us
    all_to_all x1, waiting for transfers between devices, shards(): ghosts = lax.all_to_all(ghosts, ('section', 'dp'), 0, 0, tiled=True)  7.34 us
    pallas_call x1, Pallas kernels, shards(): call(functools.partial(grads_kernel, rows, users, bound, copies), [((1, s...  6.4 us
    pallas_call x1, Pallas kernels, shards(): call(functools.partial(streams_kernel, rows, users), [((sections * parts,...  4.45 us
    unnamed x51, local copies, waits for them, and re-layouts  3.83 us
  transfers between devices with their start and end apart: 25, of which 14 were waited for; matrix products, arithmetic and copies ran while one was open for 0% of the time, Pallas kernels for 10%

profile of v1, /device:TPU:0, one launch (start us, length us, event | category | flops | bytes accessed | tf_op | source)
XLA Modules:
  0.0 119.2 jit_solution(8733694943460489288)
XLA Ops:
  0.6 2.4 %shard_map.96 = bf16[8,2,32,1024]{3,2,1,0:T(8,128)(2,1)} custom-call(bf16[4,32,8192]{2,1,0:T(8,128)(2,1)} %h_ref.3, bf16[4,32,8192]{2,1,0:T(8,128)(2,1)} %c_ref.1), custom_call_target="tpu_custom_call" | custom-call | tf_op jit(solution)/shard_map/pallas_call | solution.py:590
  3.0 7.3 %all-to-all-start = ((bf16[8,2,32,1024]{3,2,1,0:T(8,128)(2,1)}), bf16[8,2,32,1024]{3,2,1,0:T(8,128)(2,1)S(1)}, u32[]{:S(2)}, u32[]{:S(2)}) async-start(bf16[8,2,32,1024]{3,2,1,0:T(8,128)(2,1)} %shard_map.96), calls=%async_computation | async-start | bytes 2097152 | tf_op jit(solution)/shard_map/all_to_all | solution.py:44
  11.6 1.6 %collective-permute-start = (bf16[1024,128]{1,0:T(8,128)(2,1)S(1)}, bf16[1024,128]{1,0:T(8,128)(2,1)S(1)}, u32[]{:S(2)}, u32[]{:S(2)}) collective-permute-start(bf16[1024,128]{1,0:T(8,128)(2,1)S(1)} %get-tuple-element.17.refs_0_), channel_id=1, source_target_pairs={{0,16},{8,24},{16,0},{24,8},{1,17},{9,25},{17,1},{25,9},{2,18},{10... | collective-permute-start | bytes 786440 | tf_op jit(solution)/shard_map/ppermute | solution.py:40
  13.2 6.2 %collective-permute-done.refs_1_ = bf16[1024,128]{1,0:T(8,128)(2,1)S(1)} collective-permute-done((bf16[1024,128]{1,0:T(8,128)(2,1)S(1)}, bf16[1024,128]{1,0:T(8,128)(2,1)S(1)}, u32[]{:S(2)}, u32[]{:S(2)}) %collective-permute-start) | collective-permute-done | bytes 262176 | tf_op jit(solution)/shard_map/ppermute | solution.py:40
  21.0 1.7 %shard_map.97 = bf16[384,128]{1,0:T(8,128)(2,1)S(1)} custom-call(bf16[1040,128]{1,0:T(8,128)(2,1)S(1)} %get-tuple-element.18.refs_4_.down_ref, bf16[1024,128]{1,0:T(8,128)(2,1)} %copy-done.6, bf16[1024,128]{1,0:T(8,128)(2,1)S(1)} %collective-permute-done.refs_1_, bf16[1024,128]{1,0:T(8,128)(2,1)S(1)} %collective-permute-done.1.refs_2_, ...), custom_call_target="tpu_custom_call" | custom-call | tf_op jit(solution)/shard_map/pallas_call | solution.py:599
  22.8 1.8 %collective-permute-start.6 = (bf16[384,128]{1,0:T(8,128)(2,1)S(1)}, bf16[384,128]{1,0:T(8,128)(2,1)S(1)}, u32[]{:S(2)}, u32[]{:S(2)}) collective-permute-start(bf16[384,128]{1,0:T(8,128)(2,1)S(1)} %shard_map.97), channel_id=1, source_target_pairs={{0,2},{1,3},{2,0},{3,1},{4,6},{5,7},{6,4},{7,5},{8,10},{9,11},{10,... | collective-permute-start | bytes 294920 | tf_op jit(solution)/shard_map/ppermute | solution.py:40
  24.6 3.7 %collective-permute-done.3.refs_5_ = bf16[1040,128]{1,0:T(8,128)(2,1)S(1)} collective-permute-done((bf16[1040,128]{1,0:T(8,128)(2,1)S(1)}, bf16[1040,128]{1,0:T(8,128)(2,1)S(1)}, u32[]{:S(2)}, u32[]{:S(2)}) %collective-permute-start.3) | collective-permute-done | bytes 266272 | tf_op jit(solution)/shard_map/ppermute | solution.py:40
  29.5 4.6 %collective-permute-start.7 = (bf16[384,128]{1,0:T(8,128)(2,1)S(1)}, bf16[384,128]{1,0:T(8,128)(2,1)S(1)}, u32[]{:S(2)}, u32[]{:S(2)}) collective-permute-start(bf16[384,128]{1,0:T(8,128)(2,1)S(1)} %add_convert_fusion.one_ref), channel_id=1, source_target_pairs={{0,4},{1,5},{2,6},{3,7},{4,0},{5,1},{6,2},{7,3},{8,12},{9,13},{10,... | collective-permute-start | bytes 294920 | tf_op jit(solution)/shard_map/ppermute | solution.py:40
  35.6 1.6 %shard_map.95 = (bf16[4,2064,128]{2,1,0:T(8,128)(2,1)S(1)}, f32[8,128]{1,0:T(8,128)S(1)}) custom-call(bf16[1024,128]{1,0:T(8,128)(2,1)} %copy-done.6, bf16[1024,128]{1,0:T(8,128)(2,1)} %copy-done.7, bf16[1024,128]{1,0:T(8,128)(2,1)} %copy-done.8, bf16[1024,128]{1,0:T(8,128)(2,1)} %copy-done.9, bf16[1040,128]{1,0:T(8,128)(2,1)} %copy-done.5, ...), custom_call_target="tpu_custom_call" | custom-call | tf_op jit(solution)/shard_map/pallas_call | solution.py:608
  37.1 3.1 %collective-permute-done.7.two_ref = bf16[384,128]{1,0:T(8,128)(2,1)S(1)} collective-permute-done((bf16[384,128]{1,0:T(8,128)(2,1)S(1)}, bf16[384,128]{1,0:T(8,128)(2,1)S(1)}, u32[]{:S(2)}, u32[]{:S(2)}) %collective-permute-start.7) | collective-permute-done | bytes 98336 | tf_op jit(solution)/shard_map/ppermute | solution.py:40
  41.8 1.6 %shard_map.99.block_ref = bf16[8,352,128]{2,1,0:T(8,128)(2,1)S(1)} custom-call(bf16[8,2,32,1024]{3,2,1,0:T(8,128)(2,1)S(1)} %all-to-all-done.slices_ref, bf16[4,2064,128]{2,1,0:T(8,128)(2,1)S(1)} %get-tuple-element.19.packs_ref, bf16[384,128]{1,0:T(8,128)(2,1)S(1)} %shard_map.98._.sent_ref), custom_call_target="tpu_custom_call" | custom-call | tf_op jit(solution)/shard_map/pallas_call | solution.py:617
  45.9 4.2 %all-to-all-start.1 = ((bf16[8,352,128]{2,1,0:T(8,128)(2,1)}), bf16[8,352,128]{2,1,0:T(8,128)(2,1)}, u32[]{:S(2)}, u32[]{:S(2)}) async-start(bf16[8,352,128]{2,1,0:T(8,128)(2,1)} %copy-done), calls=%async_computation.1 | async-start | bytes 1441792 | tf_op jit(solution)/shard_map/all_to_all | solution.py:44
  50.1 1.6 %collective-permute-start.9 = (bf16[384,128]{1,0:T(8,128)(2,1)S(1)}, bf16[384,128]{1,0:T(8,128)(2,1)S(1)}, u32[]{:S(2)}, u32[]{:S(2)}) collective-permute-start(bf16[384,128]{1,0:T(8,128)(2,1)S(1)} %get-tuple-element.21.refs_3_), channel_id=1, source_target_pairs={{0,16},{8,24},{16,0},{24,8},{1,17},{9,25},{17,1},{25,9},{2,18},{10... | collective-permute-start | bytes 294920 | tf_op jit(solution)/shard_map/ppermute | solution.py:40
  51.8 3.0 %collective-permute-done.9._.refs_4_ = bf16[384,128]{1,0:T(8,128)(2,1)S(1)} collective-permute-done((bf16[384,128]{1,0:T(8,128)(2,1)S(1)}, bf16[384,128]{1,0:T(8,128)(2,1)S(1)}, u32[]{:S(2)}, u32[]{:S(2)}) %collective-permute-start.9) | collective-permute-done | bytes 98336 | tf_op jit(solution)/shard_map/ppermute | solution.py:40
  60.4 5.0 %collective-permute-done.10.refs_0_.block_ref = bf16[2,2,32,1024]{3,2,1,0:T(8,128)(2,1)S(1)} collective-permute-done((bf16[2,2,32,1024]{3,2,1,0:T(8,128)(2,1)S(1)}, bf16[2,2,32,1024]{3,2,1,0:T(8,128)(2,1)S(1)}, u32[]{:S(2)}, u32[]{:S(2)}) %collective-permute-start.10) | collective-permute-done | bytes 262176 | tf_op jit(solution)/shard_map/ppermute | solution.py:40
  65.6 2.2 %all-to-all-done.1.payload_ref = bf16[8,352,128]{2,1,0:T(8,128)(2,1)} async-done(((bf16[8,352,128]{2,1,0:T(8,128)(2,1)}), bf16[8,352,128]{2,1,0:T(8,128)(2,1)}, u32[]{:S(2)}, u32[]{:S(2)}) %all-to-all-start.1) | async-done | bytes 720928 | tf_op jit(solution)/shard_map/all_to_all | solution.py:44
  67.8 3.8 %shard_map.102 = bf16[8,288,128]{2,1,0:T(8,128)(2,1)S(1)} custom-call(f32[32,128]{1,0:T(8,128)} %copy-done.14, bf16[8,352,128]{2,1,0:T(8,128)(2,1)} %all-to-all-done.1.payload_ref, bf16[2,2,32,1024]{3,2,1,0:T(8,128)(2,1)} %copy-done.1, bf16[2,2,32,1024]{3,2,1,0:T(8,128)(2,1)} %copy-done.17, bf16[6,2,32,1024]{3,2,1,0:T(8,128)(2,1)} %collective-permute-done.12.refs_2_.refs_6_, ...), custom_call_target="tpu_custom_call" | custom-call | tf_op jit(solution)/shard_map/pallas_call | solution.py:641
  72.4 4.3 %all-to-all-start.2 = ((bf16[8,288,128]{2,1,0:T(8,128)(2,1)}), bf16[8,288,128]{2,1,0:T(8,128)(2,1)}, u32[]{:S(2)}, u32[]{:S(2)}) async-start(bf16[8,288,128]{2,1,0:T(8,128)(2,1)} %copy-done.4), calls=%async_computation.2 | async-start | bytes 1179648 | tf_op jit(solution)/shard_map/all_to_all | solution.py:44
  78.2 13.9 %all-to-all-done.2.states_ref = bf16[8,288,128]{2,1,0:T(8,128)(2,1)} async-done(((bf16[8,288,128]{2,1,0:T(8,128)(2,1)}), bf16[8,288,128]{2,1,0:T(8,128)(2,1)}, u32[]{:S(2)}, u32[]{:S(2)}) %all-to-all-start.2) | async-done | bytes 589856 | tf_op jit(solution)/shard_map/all_to_all | solution.py:44
  93.7 4.5 %shard_map.103 = (f32[32,1,128]{2,1,0:T(1,128)}, bf16[8,288,128]{2,1,0:T(8,128)(2,1)}) custom-call(bf16[8,2,32,1024]{3,2,1,0:T(8,128)(2,1)S(1)} %all-to-all-done.slices_ref, bf16[4,2064,128]{2,1,0:T(8,128)(2,1)S(1)} %get-tuple-element.19.packs_ref, bf16[8,288,128]{2,1,0:T(8,128)(2,1)} %all-to-all-done.2.states_ref), custom_call_target="tpu_custom_call" | custom-call | tf_op jit(solution)/shard_map/pallas_call | solution.py:654
  98.1 2.7 %all-to-all-start.3 = ((f32[32,1,128]{2,1,0:T(1,128)}), f32[32,1,128]{2,1,0:T(1,128)S(1)}, u32[]{:S(2)}, u32[]{:S(2)}) async-start(f32[32,1,128]{2,1,0:T(1,128)} %get-tuple-element.26), calls=%async_computation.3 | async-start | bytes 32768 | tf_op jit(solution)/shard_map/all_to_all | solution.py:665
  100.9 7.3 %all-to-all-done.3._ = f32[32,1,128]{2,1,0:T(1,128)S(1)} async-done(((f32[32,1,128]{2,1,0:T(1,128)}), f32[32,1,128]{2,1,0:T(1,128)S(1)}, u32[]{:S(2)}, u32[]{:S(2)}) %all-to-all-start.3) | async-done | bytes 16416 | tf_op jit(solution)/shard_map/all_to_all | solution.py:665
  109.3 2.0 %collective-permute-done.15.refs_3_ = bf16[2,2,32,1024]{3,2,1,0:T(8,128)(2,1)S(1)} collective-permute-done((bf16[2,2,32,1024]{3,2,1,0:T(8,128)(2,1)S(1)}, bf16[2,2,32,1024]{3,2,1,0:T(8,128)(2,1)S(1)}, u32[]{:S(2)}, u32[]{:S(2)}) %collective-permute-start.15) | collective-permute-done | bytes 262176 | tf_op jit(solution)/shard_map/ppermute | solution.py:40
  112.8 6.4 %shard_map.108 = (f32[1,1024,128]{2,1,0:T(8,128)}, f32[1,128,1024]{2,1,0:T(8,128)}, f32[2,4]{1,0:T(2,128)}) custom-call(bf16[4,2064,128]{2,1,0:T(8,128)(2,1)S(1)} %get-tuple-element.19.packs_ref, bf16[2,2,32,1024]{3,2,1,0:T(8,128)(2,1)} %copy-done.12, bf16[2,2,32,1024]{3,2,1,0:T(8,128)(2,1)} %copy-done.3, bf16[2,2,32,1024]{3,2,1,0:T(8,128)(2,1)} %copy-done.17, ...), custom_call_target="tpu_custom_call" | custom-call | tf_op jit(solution)/shard_map/pallas_call | solution.py:675
  (93 shorter events, 21.6 us)
Async XLA Ops:
  3.0 38.8 %all-to-all-start = ((bf16[8,2,32,1024]{3,2,1,0:T(8,128)(2,1)}), bf16[8,2,32,1024]{3,2,1,0:T(8,128)(2,1)S(1)}, u32[]{:S(2)}, u32[]{:S(2)}) async-start(bf16[8,2,32,1024]{3,2,1,0:T(8,128)(2,1)} %shard_map.96), calls=%async_computation | async-start | bytes 2097152 | tf_op jit(solution)/shard_map/all_to_all | solution.py:44
  11.6 7.8 %collective-permute-start = (bf16[1024,128]{1,0:T(8,128)(2,1)S(1)}, bf16[1024,128]{1,0:T(8,128)(2,1)S(1)}, u32[]{:S(2)}, u32[]{:S(2)}) collective-permute-start(bf16[1024,128]{1,0:T(8,128)(2,1)S(1)} %get-tuple-element.17.refs_0_), channel_id=1, source_target_pairs={{0,16},{8,24},{16,0},{24,8},{1,17},{9,25},{17,1},{25,9},{2,18},{10... | collective-permute-start | bytes 786440 | tf_op jit(solution)/shard_map/ppermute | solution.py:40
  13.2 7.8 %collective-permute-start.1 = (bf16[1024,128]{1,0:T(8,128)(2,1)S(1)}, bf16[1024,128]{1,0:T(8,128)(2,1)S(1)}, u32[]{:S(2)}, u32[]{:S(2)}) collective-permute-start(bf16[1024,128]{1,0:T(8,128)(2,1)S(1)} %get-tuple-element.17.refs_0_), channel_id=1, source_target_pairs={{0,8},{8,0},{16,24},{24,16},{1,9},{9,1},{17,25},{25,17},{2,10},{10... | collective-permute-start | bytes 786440 | tf_op jit(solution)/shard_map/ppermute | solution.py:40
  19.5 8.8 %collective-permute-start.3 = (bf16[1040,128]{1,0:T(8,128)(2,1)S(1)}, bf16[1040,128]{1,0:T(8,128)(2,1)S(1)}, u32[]{:S(2)}, u32[]{:S(2)}) collective-permute-start(bf16[1040,128]{1,0:T(8,128)(2,1)S(1)} %get-tuple-element.18.refs_4_.down_ref), channel_id=1, source_target_pairs={{0,16},{8,24},{16,0},{24,8},{1,17},{9,25},{17,1},{25,9},{2,18},{10... | collective-permute-start | bytes 798728 | tf_op jit(solution)/shard_map/ppermute | solution.py:40
  22.8 6.8 %collective-permute-start.6 = (bf16[384,128]{1,0:T(8,128)(2,1)S(1)}, bf16[384,128]{1,0:T(8,128)(2,1)S(1)}, u32[]{:S(2)}, u32[]{:S(2)}) collective-permute-start(bf16[384,128]{1,0:T(8,128)(2,1)S(1)} %shard_map.97), channel_id=1, source_target_pairs={{0,2},{1,3},{2,0},{3,1},{4,6},{5,7},{6,4},{7,5},{8,10},{9,11},{10,... | collective-permute-start | bytes 294920 | tf_op jit(solution)/shard_map/ppermute | solution.py:40
  24.6 9.6 %collective-permute-start.4 = (bf16[1040,128]{1,0:T(8,128)(2,1)S(1)}, bf16[1040,128]{1,0:T(8,128)(2,1)S(1)}, u32[]{:S(2)}, u32[]{:S(2)}) collective-permute-start(bf16[1040,128]{1,0:T(8,128)(2,1)S(1)} %get-tuple-element.18.refs_4_.down_ref), channel_id=1, source_target_pairs={{0,8},{8,0},{16,24},{24,16},{1,9},{9,1},{17,25},{25,17},{2,10},{10... | collective-permute-start | bytes 798728 | tf_op jit(solution)/shard_map/ppermute | solution.py:40
  28.3 5.9 %collective-permute-start.5 = (bf16[1040,128]{1,0:T(8,128)(2,1)S(1)}, bf16[1040,128]{1,0:T(8,128)(2,1)S(1)}, u32[]{:S(2)}, u32[]{:S(2)}) collective-permute-start(bf16[1040,128]{1,0:T(8,128)(2,1)S(1)} %collective-permute-done.3.refs_5_), channel_id=1, source_target_pairs={{0,8},{8,0},{16,24},{24,16},{1,9},{9,1},{17,25},{25,17},{2,10},{10... | collective-permute-start | bytes 798728 | tf_op jit(solution)/shard_map/ppermute | solution.py:40
  29.5 10.8 %collective-permute-start.7 = (bf16[384,128]{1,0:T(8,128)(2,1)S(1)}, bf16[384,128]{1,0:T(8,128)(2,1)S(1)}, u32[]{:S(2)}, u32[]{:S(2)}) collective-permute-start(bf16[384,128]{1,0:T(8,128)(2,1)S(1)} %add_convert_fusion.one_ref), channel_id=1, source_target_pairs={{0,4},{1,5},{2,6},{3,7},{4,0},{5,1},{6,2},{7,3},{8,12},{9,13},{10,... | collective-permute-start | bytes 294920 | tf_op jit(solution)/shard_map/ppermute | solution.py:40
  40.3 4.7 %collective-permute-start.8 = (bf16[384,128]{1,0:T(8,128)(2,1)S(1)}, bf16[384,128]{1,0:T(8,128)(2,1)S(1)}, u32[]{:S(2)}, u32[]{:S(2)}) collective-permute-start(bf16[384,128]{1,0:T(8,128)(2,1)S(1)} %shard_map.98._.sent_ref), channel_id=1, source_target_pairs={{0,1},{1,0},{2,3},{3,2},{4,5},{5,4},{6,7},{7,6},{8,9},{9,8},{10,11... | collective-permute-start | bytes 294920 | tf_op jit(solution)/shard_map/ppermute | solution.py:40
  45.9 21.9 %all-to-all-start.1 = ((bf16[8,352,128]{2,1,0:T(8,128)(2,1)}), bf16[8,352,128]{2,1,0:T(8,128)(2,1)}, u32[]{:S(2)}, u32[]{:S(2)}) async-start(bf16[8,352,128]{2,1,0:T(8,128)(2,1)} %copy-done), calls=%async_computation.1 | async-start | bytes 1441792 | tf_op jit(solution)/shard_map/all_to_all | solution.py:44
  50.1 4.7 %collective-permute-start.9 = (bf16[384,128]{1,0:T(8,128)(2,1)S(1)}, bf16[384,128]{1,0:T(8,128)(2,1)S(1)}, u32[]{:S(2)}, u32[]{:S(2)}) collective-permute-start(bf16[384,128]{1,0:T(8,128)(2,1)S(1)} %get-tuple-element.21.refs_3_), channel_id=1, source_target_pairs={{0,16},{8,24},{16,0},{24,8},{1,17},{9,25},{17,1},{25,9},{2,18},{10... | collective-permute-start | bytes 294920 | tf_op jit(solution)/shard_map/ppermute | solution.py:40
  56.8 8.8 %collective-permute-start.12 = (bf16[6,2,32,1024]{3,2,1,0:T(8,128)(2,1)S(1)}, bf16[6,2,32,1024]{3,2,1,0:T(8,128)(2,1)}, u32[]{:S(2)}, u32[]{:S(2)}) collective-permute-start(bf16[6,2,32,1024]{3,2,1,0:T(8,128)(2,1)S(1)} %get-tuple-element.25.refs_4_), channel_id=1, source_target_pairs={{0,8},{8,0},{16,24},{24,16},{1,9},{9,1},{17,25},{25,17},{2,10},{10... | collective-permute-start | bytes 2359304 | tf_op jit(solution)/shard_map/ppermute | solution.py:40
  56.8 3.7 %collective-permute-start.11 = (bf16[2,2,32,1024]{3,2,1,0:T(8,128)(2,1)S(1)}, bf16[2,2,32,1024]{3,2,1,0:T(8,128)(2,1)S(1)}, u32[]{:S(2)}, u32[]{:S(2)}) collective-permute-start(bf16[2,2,32,1024]{3,2,1,0:T(8,128)(2,1)S(1)} %get-tuple-element.22.refs_0_), channel_id=1, source_target_pairs={{0,8},{8,0},{16,24},{24,16},{1,9},{9,1},{17,25},{25,17},{2,10},{10... | collective-permute-start | bytes 786440 | tf_op jit(solution)/shard_map/ppermute | solution.py:40
  57.3 8.2 %collective-permute-start.10 = (bf16[2,2,32,1024]{3,2,1,0:T(8,128)(2,1)S(1)}, bf16[2,2,32,1024]{3,2,1,0:T(8,128)(2,1)S(1)}, u32[]{:S(2)}, u32[]{:S(2)}) collective-permute-start(bf16[2,2,32,1024]{3,2,1,0:T(8,128)(2,1)S(1)} %get-tuple-element.22.refs_0_), channel_id=1, source_target_pairs={{0,16},{8,24},{16,0},{24,8},{1,17},{9,25},{17,1},{25,9},{2,18},{10... | collective-permute-start | bytes 786440 | tf_op jit(solution)/shard_map/ppermute | solution.py:40
  58.8 1.6 %collective-permute-start.13 = (bf16[384,128]{1,0:T(8,128)(2,1)}, bf16[384,128]{1,0:T(8,128)(2,1)S(1)}, u32[]{:S(2)}, u32[]{:S(2)}) collective-permute-start(bf16[384,128]{1,0:T(8,128)(2,1)} %copy-done.13), channel_id=1, source_target_pairs={{0,8},{8,0},{16,24},{24,16},{1,9},{9,1},{17,25},{25,17},{2,10},{10... | collective-permute-start | bytes 294920 | tf_op jit(solution)/shard_map/ppermute | solution.py:40
  58.8 1.6 %collective-permute-start.14 = (bf16[384,128]{1,0:T(8,128)(2,1)S(1)}, bf16[384,128]{1,0:T(8,128)(2,1)S(1)}, u32[]{:S(2)}, u32[]{:S(2)}) collective-permute-start(bf16[384,128]{1,0:T(8,128)(2,1)S(1)} %collective-permute-done.9._.refs_4_), channel_id=1, source_target_pairs={{0,8},{8,0},{16,24},{24,16},{1,9},{9,1},{17,25},{25,17},{2,10},{10... | collective-permute-start | bytes 294920 | tf_op jit(solution)/shard_map/ppermute | solution.py:40
  72.4 19.8 %all-to-all-start.2 = ((bf16[8,288,128]{2,1,0:T(8,128)(2,1)}), bf16[8,288,128]{2,1,0:T(8,128)(2,1)}, u32[]{:S(2)}, u32[]{:S(2)}) async-start(bf16[8,288,128]{2,1,0:T(8,128)(2,1)} %copy-done.4), calls=%async_computation.2 | async-start | bytes 1179648 | tf_op jit(solution)/shard_map/all_to_all | solution.py:44
  76.7 24.2 %collective-permute-start.16 = (bf16[6,2,32,1024]{3,2,1,0:T(8,128)(2,1)}, bf16[6,2,32,1024]{3,2,1,0:T(8,128)(2,1)}, u32[]{:S(2)}, u32[]{:S(2)}) collective-permute-start(bf16[6,2,32,1024]{3,2,1,0:T(8,128)(2,1)} %copy-done.10), channel_id=1, source_target_pairs={{0,16},{8,24},{16,0},{24,8},{1,17},{9,25},{17,1},{25,9},{2,18},{10... | collective-permute-start | bytes 2359304 | tf_op jit(solution)/shard_map/ppermute | solution.py:40
  92.1 16.6 %collective-permute-start.18 = (bf16[8,288,128]{2,1,0:T(8,128)(2,1)}, bf16[8,288,128]{2,1,0:T(8,128)(2,1)}, u32[]{:S(2)}, u32[]{:S(2)}) collective-permute-start(bf16[8,288,128]{2,1,0:T(8,128)(2,1)} %all-to-all-done.2.states_ref), channel_id=1, source_target_pairs={{0,16},{8,24},{16,0},{24,8},{1,17},{9,25},{17,1},{25,9},{2,18},{10... | collective-permute-start | bytes 1769480 | tf_op jit(solution)/shard_map/ppermute | solution.py:40
  98.1 10.1 %all-to-all-start.3 = ((f32[32,1,128]{2,1,0:T(1,128)}), f32[32,1,128]{2,1,0:T(1,128)S(1)}, u32[]{:S(2)}, u32[]{:S(2)}) async-start(f32[32,1,128]{2,1,0:T(1,128)} %get-tuple-element.26), calls=%async_computation.3 | async-start | bytes 32768 | tf_op jit(solution)/shard_map/all_to_all | solution.py:665
  108.2 3.7 %collective-permute-start.17 = (bf16[6,2,32,1024]{3,2,1,0:T(8,128)(2,1)}, bf16[6,2,32,1024]{3,2,1,0:T(8,128)(2,1)S(1)}, u32[]{:S(2)}, u32[]{:S(2)}) collective-permute-start(bf16[6,2,32,1024]{3,2,1,0:T(8,128)(2,1)} %shard_map.105.refs_5_), channel_id=1, source_target_pairs={{0,8},{8,0},{16,24},{24,16},{1,9},{9,1},{17,25},{25,17},{2,10},{10... | collective-permute-start | bytes 2359304 | tf_op jit(solution)/shard_map/ppermute | solution.py:40
  108.3 3.6 %collective-permute-start.19 = (bf16[8,288,128]{2,1,0:T(8,128)(2,1)}, bf16[8,288,128]{2,1,0:T(8,128)(2,1)S(1)}, u32[]{:S(2)}, u32[]{:S(2)}) collective-permute-start(bf16[8,288,128]{2,1,0:T(8,128)(2,1)} %shard_map.106.refs_8_), channel_id=1, source_target_pairs={{0,8},{8,0},{16,24},{24,16},{1,9},{9,1},{17,25},{25,17},{2,10},{10... | collective-permute-start | bytes 1769480 | tf_op jit(solution)/shard_map/ppermute | solution.py:40
  108.7 4.0 %collective-permute-start.20 = (bf16[8,288,128]{2,1,0:T(8,128)(2,1)}, bf16[8,288,128]{2,1,0:T(8,128)(2,1)S(1)}, u32[]{:S(2)}, u32[]{:S(2)}) collective-permute-start(bf16[8,288,128]{2,1,0:T(8,128)(2,1)} %shard_map.107.refs_9_), channel_id=1, source_target_pairs={{0,8},{8,0},{16,24},{24,16},{1,9},{9,1},{17,25},{25,17},{2,10},{10... | collective-permute-start | bytes 1769480 | tf_op jit(solution)/shard_map/ppermute | solution.py:40
  108.8 2.4 %collective-permute-start.15 = (bf16[2,2,32,1024]{3,2,1,0:T(8,128)(2,1)S(1)}, bf16[2,2,32,1024]{3,2,1,0:T(8,128)(2,1)S(1)}, u32[]{:S(2)}, u32[]{:S(2)}) collective-permute-start(bf16[2,2,32,1024]{3,2,1,0:T(8,128)(2,1)S(1)} %shard_map.104.refs_1_), channel_id=1, source_target_pairs={{0,8},{8,0},{16,24},{24,16},{1,9},{9,1},{17,25},{25,17},{2,10},{10... | collective-permute-start | bytes 786440 | tf_op jit(solution)/shard_map/ppermute | solution.py:40
  (26 other events, 179.1 us)

commit v2 on v1

--- a/solution.py
+++ b/solution.py
@@ -195,21 +195,6 @@
     del block_ref, out_ref
 
 
-def add_tie_kernel(block_ref, sent_ref, came_ref, out_ref, sum_ref):
-    del block_ref, out_ref
-    sum_ref[...] = (sent_ref[...].astype(F32) + came_ref[...].astype(F32)).astype(BF16)
-
-
-def add_tie(block, sent, came):
-    return call(
-        add_tie_kernel,
-        [(block.shape, block.dtype), (sent.shape, sent.dtype)],
-        [ANY, VMEM, VMEM],
-        out_specs=[ANY, VMEM],
-        input_output_aliases={0: 0},
-    )(block, sent, came)
-
-
 def tie(block, after):
     return call(
         tie_kernel,
@@ -254,7 +239,8 @@
     out_ref[...] = (one_ref[...].astype(F32) + two_ref[...].astype(F32)).astype(BF16)
 
 
-def project_kernel(slices_ref, packs_ref, _, out_ref):
+def project_kernel(slices_ref, packs_ref, _, out_ref, token_ref):
+    token_ref[...] = jnp.zeros_like(token_ref)
     parts, _, own, slab = slices_ref.shape
     sections, _, rank = packs_ref.shape
     slice_h = slices_ref[:, 0].reshape(parts * own, slab)
@@ -275,10 +261,10 @@
 
 def solve_kernel(width, notes_far, payload_ref, *refs):
     *pieces, out_ref, gram_ref, notes_ref, sems = refs
-    pieces = pieces[3:]
     own = notes_ref.shape[0]
     parts, size, rank = out_ref.shape
     layers = (size // own - 1) // 2
+    pieces = pieces[-layers:]
     each = gram_ref.shape[0] // layers
     section = lax.axis_index("section")
     copies = [pltpu.make_async_copy(notes_far, notes_ref, sems.at[layers])]
@@ -374,21 +360,23 @@
 
 
 def streams_kernel(
-    rows, users, slices_ref, packs_ref, states_ref, ghosts_ref, passed_ref, streams_ref, sem
+    rows, users, slices_ref, packs_ref, states_ref, ghosts_ref, streams_ref, held_ref, sems
 ):
     parts, _, own, slab = slices_ref.shape
     layers, _, rank = packs_ref.shape
     everyone = parts * own
     counts = (parts, own // rows, rows)
-    passing = pltpu.make_async_copy(states_ref, passed_ref, sem)
-    passing.start()
+    halves = [pl.ds(0, layers * own), pl.ds(layers * own, (layers + 1) * own)]
+    copies = [
+        pltpu.make_async_copy(states_ref.at[:, half], held_ref.at[:, half], sems.at[i])
+        for i, half in enumerate(halves)
+    ]
+    for copy in copies:
+        copy.start()
 
     def state(index):
-        return state_rows(states_ref, index, own)
-
-    extra = state(2 * layers)
-    columns = [(2 * layers,)] + [(l, layers + l) for l in range(1, layers)]
-    ids, *alphas = spread(extra, columns)
+        return state_rows(held_ref, index, own)
+
     step = rows
     while step < 256 and everyone % (2 * step) == 0:
         step *= 2
@@ -398,13 +386,20 @@
     wide = stream.astype(F32)
     for l in range(layers):
         streams_ref[l] = stream
+        normed = (wide * gain_of(packs_ref, l, slab)).astype(BF16)
+        grams = [dot_last(normed[here], normed[here]) for here in spans]
+        if l == 0:
+            for copy in copies:
+                copy.wait()
         low, scaled = state(l), state(layers + l)
-        normed = (wide * gain_of(packs_ref, l, slab)).astype(BF16)
         for at, here in enumerate(spans):
-            pairs[at] += dot_last(normed[here], normed[here]) * dot_last(scaled[here], scaled[here])
+            pairs[at] += grams[at] * dot_last(scaled[here], scaled[here])
         if l < layers - 1:
             wide = wide + dot(low, up_of(packs_ref, l, slab))
             stream = wide.astype(BF16)
+    extra = state(2 * layers)
+    columns = [(2 * layers,)] + [(l, layers + l) for l in range(1, layers)]
+    ids, *alphas = spread(extra, columns)
     delta = slices_ref[:, 1].reshape(everyone, slab)
     wide = delta.astype(F32)
     for l in range(layers - 1, -1, -1):
@@ -431,8 +426,6 @@
         mine = user_lanes(ids, counts, users, lanes, m)
         total = jnp.sum(jnp.where(mine, rowsum, 0.0), 0, keepdims=True)
         ghosts_ref[:, m : m + 1, :] = jnp.broadcast_to(total[None], (copies, 1, lanes))
-    passing.wait()
-
 
 def grads_kernel(rows, users, bound, copies, packs_ref, *refs):
     count = (len(refs) - 12) // 3
@@ -614,15 +607,15 @@
     )(*in_hbm(*ups, *downs))
     sent, came = sum_parts(gram, token)
 
-    (payload,) = call(
+    payload, token = call(
         project_kernel,
-        [((parts, (3 * layers - 1) * own, rank), BF16)],
+        [((parts, (3 * layers - 1) * own, rank), BF16), ((8, LANES), F32)],
         [VMEM, VMEM, ANY],
     )(slices, *in_vmem(packs), sent)
-    payload, gram = add_tie(payload, sent, came)
     payload = exchange(payload)
+    gram = (sent.astype(F32) + came.astype(F32)).astype(BF16)
     grams = gather(gram)
-    cut = max(1, parts * 2 // 8)
+    cut = max(1, parts * 3 // 8)
     one, two, notes = call(
         functools.partial(notes_kernel, copies),
         [
@@ -630,44 +623,43 @@
             ((parts - cut, 2, own, slab), BF16),
             ((own, LANES), F32),
         ],
-        [VMEM, FAR, VMEM, VMEM, ANY],
+        [VMEM, FAR, VMEM, VMEM, VMEM],
         scratch_shapes=[pltpu.VMEM((share, rows, width), BF16), pltpu.SemaphoreType.DMA],
-    )(slices, *in_hbm(hidden_in), user_of_row, included, grams[1])
-    ones = gather_far(one, copies)
+    )(slices, *in_hbm(hidden_in), user_of_row, included, token)
+    ones = gather(one, copies)
     twos = gather_far(two, copies)
-    ones_own, twos_own = swap(one, "section", copies), swap(two, "section", copies)
-    count = 2 * len(ones)
+    twos_own = swap(two, "section", copies)
+    count = len(ones)
 
     (state,) = call(
         functools.partial(solve_kernel, width),
         [((parts, (2 * layers + 1) * own, rank), BF16)],
-        [FAR, VMEM] + [FAR] * (3 + len(grams)),
+        [FAR, VMEM] + [FAR] * (count + len(grams)),
         scratch_shapes=[
             pltpu.VMEM((layers * each, rank), BF16),
             pltpu.VMEM((own, LANES), F32),
             pltpu.SemaphoreType.DMA((layers + 1,)),
         ],
-    )(*in_hbm(notes), payload, *in_hbm(ones[1], ones_own, twos_own, *grams))
+    )(*in_hbm(notes), payload, *in_hbm(*ones[1:], twos_own, *grams))
     states = exchange(state)
 
     lanes = -(-users * parts // LANES) * LANES
-    ghosts, mine = call(
+    (ghosts,) = call(
         functools.partial(streams_kernel, rows, users),
-        [((sections * parts, share, lanes), F32), (states.shape, BF16)],
-        [VMEM] * 3,
-        out_specs=[VMEM, FAR],
+        [((sections * parts, share, lanes), F32)],
+        [VMEM, VMEM, FAR],
+        limit=LIMIT + 4 * states.size,
         scratch_shapes=[
             pltpu.VMEM((layers, everyone, slab), BF16),
-            pltpu.SemaphoreType.DMA,
+            pltpu.VMEM(states.shape, BF16),
+            pltpu.SemaphoreType.DMA((2,)),
         ],
-    )(slices, *in_vmem(packs), states)
+    )(slices, *in_vmem(packs), *in_hbm(states))
     states_far = gather_far(states, copies)
     ghosts = lax.all_to_all(ghosts, ("section", "dp"), 0, 0, tiled=True)
-    ones = ones[:1] + [tie(piece, ghosts) for piece in ones[1:]]
     twos = twos[:1] + [tie(piece, ghosts) for piece in twos[1:]]
-    ones = ones + [ones_own] + [swap(piece, "section", copies) for piece in ones[1:]]
     twos = twos + [twos_own] + [swap(piece, "section", copies) for piece in twos[1:]]
-    states = [tie(mine, ghosts)] + [tie(piece, ghosts) for piece in states_far[1:]]
+    states = states_far[:1] + [tie(piece, ghosts) for piece in states_far[1:]]
     states = states + [swap(piece, "section", copies) for piece in states]
     ghosts = ghosts.reshape(sections, parts, share, lanes)
     bound = 0.8 * math.sqrt(sections * (rows // users) * width * width)

time: 120 us -> 120 us (level)
  waiting for transfers between devices: 52.1 us -> 50.9 us
    all_to_all x3, starting transfers between devices: 15.8 us -> 17.2 us  [exchange(): return lax.all_to_all(blocks, 'dp', 0, 0, tiled=True)]
    all_to_all x3, waiting for transfers between devices: 16.2 us -> 14.8 us  [exchange(): return lax.all_to_all(blocks, 'dp', 0, 0, tiled=True)]
    unnamed x51 -> x47, local copies, waits for them, and re-layouts: 3.83 us -> 4.87 us
  transfers between devices with their start and end apart: 25 -> 25, of which waited for: 14 -> 11; matrix products, arithmetic and copies ran while one was open for 0% -> 0% of each run, Pallas kernels for 10% -> 8%
where the time goes in v2:
time: 120 us
  waiting for transfers between devices  50.9 us (42%)
  starting transfers between devices  38.5 us (32%)
  Pallas kernels  24.3 us (20%)
  local copies, waits for them, and re-layouts  4.87 us (4%)
    ppermute x21, waiting for transfers between devices, swap(): return lax.ppermute(block, axis, [(i, i ^ bit) for i in range(size)])  29.1 us
    ppermute x21, starting transfers between devices, swap(): return lax.ppermute(block, axis, [(i, i ^ bit) for i in range(size)])  18.6 us
    all_to_all x3, starting transfers between devices, exchange(): return lax.all_to_all(blocks, 'dp', 0, 0, tiled=True)  17.2 us
    all_to_all x3, waiting for transfers between devices, exchange(): return lax.all_to_all(blocks, 'dp', 0, 0, tiled=True)  14.8 us
    all_to_all x1, waiting for transfers between devices, shards(): ghosts = lax.all_to_all(ghosts, ('section', 'dp'), 0, 0, tiled=True)  7.03 us
    pallas_call x1, Pallas kernels, shards(): call(functools.partial(grads_kernel, rows, users, bound, copies), [((1, s...  6.38 us
    unnamed x47, local copies, waits for them, and re-layouts  4.87 us
    pallas_call x1, Pallas kernels, shards(): call(functools.partial(streams_kernel, rows, users), [((sections * parts,...  4.22 us
  transfers between devices with their start and end apart: 25, of which 11 were waited for; matrix products, arithmetic and copies ran while one was open for 0% of the time, Pallas kernels for 8%

profile of v2, /device:TPU:0, one launch (start us, length us, event | category | flops | bytes accessed | tf_op | source)
XLA Modules:
  0.0 119.6 jit_solution(2875770645520243811)
XLA Ops:
  0.6 2.4 %shard_map.96 = bf16[8,2,32,1024]{3,2,1,0:T(8,128)(2,1)} custom-call(bf16[4,32,8192]{2,1,0:T(8,128)(2,1)} %h_ref.3, bf16[4,32,8192]{2,1,0:T(8,128)(2,1)} %c_ref.1), custom_call_target="tpu_custom_call" | custom-call | tf_op jit(solution)/shard_map/pallas_call | solution.py:583
  3.0 7.3 %all-to-all-start = ((bf16[8,2,32,1024]{3,2,1,0:T(8,128)(2,1)}), bf16[8,2,32,1024]{3,2,1,0:T(8,128)(2,1)S(1)}, u32[]{:S(2)}, u32[]{:S(2)}) async-start(bf16[8,2,32,1024]{3,2,1,0:T(8,128)(2,1)} %shard_map.96), calls=%async_computation | async-start | bytes 2097152 | tf_op jit(solution)/shard_map/all_to_all | solution.py:44
  11.6 1.6 %collective-permute-start = (bf16[1024,128]{1,0:T(8,128)(2,1)S(1)}, bf16[1024,128]{1,0:T(8,128)(2,1)S(1)}, u32[]{:S(2)}, u32[]{:S(2)}) collective-permute-start(bf16[1024,128]{1,0:T(8,128)(2,1)S(1)} %get-tuple-element.15.refs_0_), channel_id=1, source_target_pairs={{0,16},{8,24},{16,0},{24,8},{1,17},{9,25},{17,1},{25,9},{2,18},{10... | collective-permute-start | bytes 786440 | tf_op jit(solution)/shard_map/ppermute | solution.py:40
  13.2 6.2 %collective-permute-done.refs_1_ = bf16[1024,128]{1,0:T(8,128)(2,1)S(1)} collective-permute-done((bf16[1024,128]{1,0:T(8,128)(2,1)S(1)}, bf16[1024,128]{1,0:T(8,128)(2,1)S(1)}, u32[]{:S(2)}, u32[]{:S(2)}) %collective-permute-start) | collective-permute-done | bytes 262176 | tf_op jit(solution)/shard_map/ppermute | solution.py:40
  21.0 1.7 %shard_map.97 = bf16[384,128]{1,0:T(8,128)(2,1)S(1)} custom-call(bf16[1040,128]{1,0:T(8,128)(2,1)S(1)} %get-tuple-element.16.refs_4_.down_ref, bf16[1024,128]{1,0:T(8,128)(2,1)} %copy-done.2, bf16[1024,128]{1,0:T(8,128)(2,1)S(1)} %collective-permute-done.refs_1_, bf16[1024,128]{1,0:T(8,128)(2,1)S(1)} %collective-permute-done.1.refs_2_, ...), custom_call_target="tpu_custom_call" | custom-call | tf_op jit(solution)/shard_map/pallas_call | solution.py:592
  22.7 1.8 %collective-permute-start.6 = (bf16[384,128]{1,0:T(8,128)(2,1)S(1)}, bf16[384,128]{1,0:T(8,128)(2,1)S(1)}, u32[]{:S(2)}, u32[]{:S(2)}) collective-permute-start(bf16[384,128]{1,0:T(8,128)(2,1)S(1)} %shard_map.97), channel_id=1, source_target_pairs={{0,2},{1,3},{2,0},{3,1},{4,6},{5,7},{6,4},{7,5},{8,10},{9,11},{10,... | collective-permute-start | bytes 294920 | tf_op jit(solution)/shard_map/ppermute | solution.py:40
  24.5 3.7 %collective-permute-done.3.refs_5_ = bf16[1040,128]{1,0:T(8,128)(2,1)S(1)} collective-permute-done((bf16[1040,128]{1,0:T(8,128)(2,1)S(1)}, bf16[1040,128]{1,0:T(8,128)(2,1)S(1)}, u32[]{:S(2)}, u32[]{:S(2)}) %collective-permute-start.3) | collective-permute-done | bytes 266272 | tf_op jit(solution)/shard_map/ppermute | solution.py:40
  29.5 4.6 %collective-permute-start.7 = (bf16[384,128]{1,0:T(8,128)(2,1)S(1)}, bf16[384,128]{1,0:T(8,128)(2,1)S(1)}, u32[]{:S(2)}, u32[]{:S(2)}) collective-permute-start(bf16[384,128]{1,0:T(8,128)(2,1)S(1)} %add_convert_fusion.1.one_ref), channel_id=1, source_target_pairs={{0,4},{1,5},{2,6},{3,7},{4,0},{5,1},{6,2},{7,3},{8,12},{9,13},{10,... | collective-permute-start | bytes 294920 | tf_op jit(solution)/shard_map/ppermute | solution.py:40
  37.1 3.1 %collective-permute-done.7.two_ref = bf16[384,128]{1,0:T(8,128)(2,1)S(1)} collective-permute-done((bf16[384,128]{1,0:T(8,128)(2,1)S(1)}, bf16[384,128]{1,0:T(8,128)(2,1)S(1)}, u32[]{:S(2)}, u32[]{:S(2)}) %collective-permute-start.7) | collective-permute-done | bytes 98336 | tf_op jit(solution)/shard_map/ppermute | solution.py:40
  40.3 1.6 %shard_map.99 = (bf16[8,352,128]{2,1,0:T(8,128)(2,1)S(1)}, f32[8,128]{1,0:T(8,128)S(1)}) custom-call(bf16[8,2,32,1024]{3,2,1,0:T(8,128)(2,1)S(1)} %all-to-all-done.slices_ref, bf16[4,2064,128]{2,1,0:T(8,128)(2,1)S(1)} %get-tuple-element.17.packs_ref, bf16[384,128]{1,0:T(8,128)(2,1)S(1)} %shard_map.98._), custom_call_target="tpu_custom_call" | custom-call | tf_op jit(solution)/shard_map/pallas_call | solution.py:610
  42.9 4.2 %all-to-all-start.1 = ((bf16[8,352,128]{2,1,0:T(8,128)(2,1)}), bf16[8,352,128]{2,1,0:T(8,128)(2,1)}, u32[]{:S(2)}, u32[]{:S(2)}) async-start(bf16[8,352,128]{2,1,0:T(8,128)(2,1)} %copy-done.6), calls=%async_computation.1 | async-start | bytes 1441792 | tf_op jit(solution)/shard_map/all_to_all | solution.py:44
  48.5 1.6 %collective-permute-start.8 = (bf16[3,2,32,1024]{3,2,1,0:T(8,128)(2,1)S(1)}, bf16[3,2,32,1024]{3,2,1,0:T(8,128)(2,1)S(1)}, u32[]{:S(2)}, u32[]{:S(2)}) collective-permute-start(bf16[3,2,32,1024]{3,2,1,0:T(8,128)(2,1)S(1)} %get-tuple-element.20.refs_0_), channel_id=1, source_target_pairs={{0,16},{8,24},{16,0},{24,8},{1,17},{9,25},{17,1},{25,9},{2,18},{10... | collective-permute-start | bytes 1179656 | tf_op jit(solution)/shard_map/ppermute | solution.py:40
  50.1 1.9 %collective-permute-start.13 = (bf16[384,128]{1,0:T(8,128)(2,1)S(1)}, bf16[384,128]{1,0:T(8,128)(2,1)S(1)}, u32[]{:S(2)}, u32[]{:S(2)}) collective-permute-start(bf16[384,128]{1,0:T(8,128)(2,1)S(1)} %shard_map.98._), channel_id=1, source_target_pairs={{0,1},{1,0},{2,3},{3,2},{4,5},{5,4},{6,7},{7,6},{8,9},{9,8},{10,11... | collective-permute-start | bytes 294920 | tf_op jit(solution)/shard_map/ppermute | solution.py:40
  52.2 6.5 %collective-permute-done.8.refs_0_.refs_1_ = bf16[3,2,32,1024]{3,2,1,0:T(8,128)(2,1)S(1)} collective-permute-done((bf16[3,2,32,1024]{3,2,1,0:T(8,128)(2,1)S(1)}, bf16[3,2,32,1024]{3,2,1,0:T(8,128)(2,1)S(1)}, u32[]{:S(2)}, u32[]{:S(2)}) %collective-permute-start.8) | collective-permute-done | bytes 393248 | tf_op jit(solution)/shard_map/ppermute | solution.py:40
  58.8 1.6 %collective-permute-start.14 = (bf16[384,128]{1,0:T(8,128)(2,1)S(1)}, bf16[384,128]{1,0:T(8,128)(2,1)S(1)}, u32[]{:S(2)}, u32[]{:S(2)}) collective-permute-start(bf16[384,128]{1,0:T(8,128)(2,1)S(1)} %add_convert_fusion.refs_4_), channel_id=1, source_target_pairs={{0,16},{8,24},{16,0},{24,8},{1,17},{9,25},{17,1},{25,9},{2,18},{10... | collective-permute-start | bytes 294920 | tf_op jit(solution)/shard_map/ppermute | solution.py:40
  60.6 3.5 %collective-permute-done.14.refs_5_ = bf16[384,128]{1,0:T(8,128)(2,1)S(1)} collective-permute-done((bf16[384,128]{1,0:T(8,128)(2,1)S(1)}, bf16[384,128]{1,0:T(8,128)(2,1)S(1)}, u32[]{:S(2)}, u32[]{:S(2)}) %collective-permute-start.14) | collective-permute-done | bytes 98336 | tf_op jit(solution)/shard_map/ppermute | solution.py:40
  67.1 3.8 %shard_map.101 = bf16[8,288,128]{2,1,0:T(8,128)(2,1)S(1)} custom-call(f32[32,128]{1,0:T(8,128)} %copy-done.9, bf16[8,352,128]{2,1,0:T(8,128)(2,1)} %all-to-all-done.1.payload_ref, bf16[3,2,32,1024]{3,2,1,0:T(8,128)(2,1)} %copy-done.13, bf16[3,2,32,1024]{3,2,1,0:T(8,128)(2,1)} %copy-done.14, bf16[3,2,32,1024]{3,2,1,0:T(8,128)(2,1)} %collective-permute-done.10.refs_2_.refs_3_, ...), custom_call_target="tpu_custom_call" | custom-call | tf_op jit(solution)/shard_map/pallas_call | solution.py:634
  71.7 5.7 %all-to-all-start.2 = ((bf16[8,288,128]{2,1,0:T(8,128)(2,1)}), bf16[8,288,128]{2,1,0:T(8,128)(2,1)}, u32[]{:S(2)}, u32[]{:S(2)}) async-start(bf16[8,288,128]{2,1,0:T(8,128)(2,1)} %copy-done), calls=%async_computation.2 | async-start | bytes 1179648 | tf_op jit(solution)/shard_map/all_to_all | solution.py:44
  78.9 14.8 %all-to-all-done.2.states_ref.refs_8_ = bf16[8,288,128]{2,1,0:T(8,128)(2,1)} async-done(((bf16[8,288,128]{2,1,0:T(8,128)(2,1)}), bf16[8,288,128]{2,1,0:T(8,128)(2,1)}, u32[]{:S(2)}, u32[]{:S(2)}) %all-to-all-start.2) | async-done | bytes 589856 | tf_op jit(solution)/shard_map/all_to_all | solution.py:44
  95.2 4.2 %shard_map.102 = f32[32,1,128]{2,1,0:T(1,128)} custom-call(bf16[8,2,32,1024]{3,2,1,0:T(8,128)(2,1)S(1)} %all-to-all-done.slices_ref, bf16[4,2064,128]{2,1,0:T(8,128)(2,1)S(1)} %get-tuple-element.17.packs_ref, bf16[8,288,128]{2,1,0:T(8,128)(2,1)} %all-to-all-done.2.states_ref.refs_8_), custom_call_target="tpu_custom_call" | custom-call | tf_op jit(solution)/shard_map/pallas_call | solution.py:647
  99.5 2.7 %all-to-all-start.3 = ((f32[32,1,128]{2,1,0:T(1,128)}), f32[32,1,128]{2,1,0:T(1,128)S(1)}, u32[]{:S(2)}, u32[]{:S(2)}) async-start(f32[32,1,128]{2,1,0:T(1,128)} %shard_map.102), calls=%async_computation.3 | async-start | bytes 32768 | tf_op jit(solution)/shard_map/all_to_all | solution.py:659
  102.2 7.0 %all-to-all-done.3._ = f32[32,1,128]{2,1,0:T(1,128)S(1)} async-done(((f32[32,1,128]{2,1,0:T(1,128)}), f32[32,1,128]{2,1,0:T(1,128)S(1)}, u32[]{:S(2)}, u32[]{:S(2)}) %all-to-all-start.3) | async-done | bytes 16416 | tf_op jit(solution)/shard_map/all_to_all | solution.py:659
  109.8 2.6 %collective-permute-done.19.refs_10_ = bf16[8,288,128]{2,1,0:T(8,128)(2,1)S(1)} collective-permute-done((bf16[8,288,128]{2,1,0:T(8,128)(2,1)}, bf16[8,288,128]{2,1,0:T(8,128)(2,1)S(1)}, u32[]{:S(2)}, u32[]{:S(2)}) %collective-permute-start.19) | collective-permute-done | bytes 589856 | tf_op jit(solution)/shard_map/ppermute | solution.py:40
  113.3 6.4 %shard_map.105 = (f32[1,1024,128]{2,1,0:T(8,128)}, f32[1,128,1024]{2,1,0:T(8,128)}, f32[2,4]{1,0:T(2,128)}) custom-call(bf16[4,2064,128]{2,1,0:T(8,128)(2,1)S(1)} %get-tuple-element.17.packs_ref, bf16[3,2,32,1024]{3,2,1,0:T(8,128)(2,1)} %copy-done.8, bf16[3,2,32,1024]{3,2,1,0:T(8,128)(2,1)} %copy-done.13, bf16[3,2,32,1024]{3,2,1,0:T(8,128)(2,1)} %copy-done.14, ...), custom_call_target="tpu_custom_call" | custom-call | tf_op jit(solution)/shard_map/pallas_call | solution.py:667
  (87 shorter events, 18.1 us)
Async XLA Ops:
  3.0 37.3 %all-to-all-start = ((bf16[8,2,32,1024]{3,2,1,0:T(8,128)(2,1)}), bf16[8,2,32,1024]{3,2,1,0:T(8,128)(2,1)S(1)}, u32[]{:S(2)}, u32[]{:S(2)}) async-start(bf16[8,2,32,1024]{3,2,1,0:T(8,128)(2,1)} %shard_map.96), calls=%async_computation | async-start | bytes 2097152 | tf_op jit(solution)/shard_map/all_to_all | solution.py:44
  11.6 7.8 %collective-permute-start = (bf16[1024,128]{1,0:T(8,128)(2,1)S(1)}, bf16[1024,128]{1,0:T(8,128)(2,1)S(1)}, u32[]{:S(2)}, u32[]{:S(2)}) collective-permute-start(bf16[1024,128]{1,0:T(8,128)(2,1)S(1)} %get-tuple-element.15.refs_0_), channel_id=1, source_target_pairs={{0,16},{8,24},{16,0},{24,8},{1,17},{9,25},{17,1},{25,9},{2,18},{10... | collective-permute-start | bytes 786440 | tf_op jit(solution)/shard_map/ppermute | solution.py:40
  13.2 7.8 %collective-permute-start.1 = (bf16[1024,128]{1,0:T(8,128)(2,1)S(1)}, bf16[1024,128]{1,0:T(8,128)(2,1)S(1)}, u32[]{:S(2)}, u32[]{:S(2)}) collective-permute-start(bf16[1024,128]{1,0:T(8,128)(2,1)S(1)} %get-tuple-element.15.refs_0_), channel_id=1, source_target_pairs={{0,8},{8,0},{16,24},{24,16},{1,9},{9,1},{17,25},{25,17},{2,10},{10... | collective-permute-start | bytes 786440 | tf_op jit(solution)/shard_map/ppermute | solution.py:40
  19.4 1.5 %collective-permute-start.2 = (bf16[1024,128]{1,0:T(8,128)(2,1)S(1)}, bf16[1024,128]{1,0:T(8,128)(2,1)S(1)}, u32[]{:S(2)}, u32[]{:S(2)}) collective-permute-start(bf16[1024,128]{1,0:T(8,128)(2,1)S(1)} %collective-permute-done.refs_1_), channel_id=1, source_target_pairs={{0,8},{8,0},{16,24},{24,16},{1,9},{9,1},{17,25},{25,17},{2,10},{10... | collective-permute-start | bytes 786440 | tf_op jit(solution)/shard_map/ppermute | solution.py:40
  19.4 8.8 %collective-permute-start.3 = (bf16[1040,128]{1,0:T(8,128)(2,1)S(1)}, bf16[1040,128]{1,0:T(8,128)(2,1)S(1)}, u32[]{:S(2)}, u32[]{:S(2)}) collective-permute-start(bf16[1040,128]{1,0:T(8,128)(2,1)S(1)} %get-tuple-element.16.refs_4_.down_ref), channel_id=1, source_target_pairs={{0,16},{8,24},{16,0},{24,8},{1,17},{9,25},{17,1},{25,9},{2,18},{10... | collective-permute-start | bytes 798728 | tf_op jit(solution)/shard_map/ppermute | solution.py:40
  22.7 6.8 %collective-permute-start.6 = (bf16[384,128]{1,0:T(8,128)(2,1)S(1)}, bf16[384,128]{1,0:T(8,128)(2,1)S(1)}, u32[]{:S(2)}, u32[]{:S(2)}) collective-permute-start(bf16[384,128]{1,0:T(8,128)(2,1)S(1)} %shard_map.97), channel_id=1, source_target_pairs={{0,2},{1,3},{2,0},{3,1},{4,6},{5,7},{6,4},{7,5},{8,10},{9,11},{10,... | collective-permute-start | bytes 294920 | tf_op jit(solution)/shard_map/ppermute | solution.py:40
  24.5 9.6 %collective-permute-start.4 = (bf16[1040,128]{1,0:T(8,128)(2,1)S(1)}, bf16[1040,128]{1,0:T(8,128)(2,1)S(1)}, u32[]{:S(2)}, u32[]{:S(2)}) collective-permute-start(bf16[1040,128]{1,0:T(8,128)(2,1)S(1)} %get-tuple-element.16.refs_4_.down_ref), channel_id=1, source_target_pairs={{0,8},{8,0},{16,24},{24,16},{1,9},{9,1},{17,25},{25,17},{2,10},{10... | collective-permute-start | bytes 798728 | tf_op jit(solution)/shard_map/ppermute | solution.py:40
  28.2 5.9 %collective-permute-start.5 = (bf16[1040,128]{1,0:T(8,128)(2,1)S(1)}, bf16[1040,128]{1,0:T(8,128)(2,1)S(1)}, u32[]{:S(2)}, u32[]{:S(2)}) collective-permute-start(bf16[1040,128]{1,0:T(8,128)(2,1)S(1)} %collective-permute-done.3.refs_5_), channel_id=1, source_target_pairs={{0,8},{8,0},{16,24},{24,16},{1,9},{9,1},{17,25},{25,17},{2,10},{10... | collective-permute-start | bytes 798728 | tf_op jit(solution)/shard_map/ppermute | solution.py:40
  29.5 10.8 %collective-permute-start.7 = (bf16[384,128]{1,0:T(8,128)(2,1)S(1)}, bf16[384,128]{1,0:T(8,128)(2,1)S(1)}, u32[]{:S(2)}, u32[]{:S(2)}) collective-permute-start(bf16[384,128]{1,0:T(8,128)(2,1)S(1)} %add_convert_fusion.1.one_ref), channel_id=1, source_target_pairs={{0,4},{1,5},{2,6},{3,7},{4,0},{5,1},{6,2},{7,3},{8,12},{9,13},{10,... | collective-permute-start | bytes 294920 | tf_op jit(solution)/shard_map/ppermute | solution.py:40
  42.9 24.2 %all-to-all-start.1 = ((bf16[8,352,128]{2,1,0:T(8,128)(2,1)}), bf16[8,352,128]{2,1,0:T(8,128)(2,1)}, u32[]{:S(2)}, u32[]{:S(2)}) async-start(bf16[8,352,128]{2,1,0:T(8,128)(2,1)} %copy-done.6), calls=%async_computation.1 | async-start | bytes 1441792 | tf_op jit(solution)/shard_map/all_to_all | solution.py:44
  48.5 10.2 %collective-permute-start.8 = (bf16[3,2,32,1024]{3,2,1,0:T(8,128)(2,1)S(1)}, bf16[3,2,32,1024]{3,2,1,0:T(8,128)(2,1)S(1)}, u32[]{:S(2)}, u32[]{:S(2)}) collective-permute-start(bf16[3,2,32,1024]{3,2,1,0:T(8,128)(2,1)S(1)} %get-tuple-element.20.refs_0_), channel_id=1, source_target_pairs={{0,16},{8,24},{16,0},{24,8},{1,17},{9,25},{17,1},{25,9},{2,18},{10... | collective-permute-start | bytes 1179656 | tf_op jit(solution)/shard_map/ppermute | solution.py:40
  50.1 15.3 %collective-permute-start.12 = (bf16[5,2,32,1024]{3,2,1,0:T(8,128)(2,1)S(1)}, bf16[5,2,32,1024]{3,2,1,0:T(8,128)(2,1)S(1)}, u32[]{:S(2)}, u32[]{:S(2)}) collective-permute-start(bf16[5,2,32,1024]{3,2,1,0:T(8,128)(2,1)S(1)} %get-tuple-element.21.refs_4_), channel_id=1, source_target_pairs={{0,8},{8,0},{16,24},{24,16},{1,9},{9,1},{17,25},{25,17},{2,10},{10... | collective-permute-start | bytes 1966088 | tf_op jit(solution)/shard_map/ppermute | solution.py:40
  50.1 8.6 %collective-permute-start.13 = (bf16[384,128]{1,0:T(8,128)(2,1)S(1)}, bf16[384,128]{1,0:T(8,128)(2,1)S(1)}, u32[]{:S(2)}, u32[]{:S(2)}) collective-permute-start(bf16[384,128]{1,0:T(8,128)(2,1)S(1)} %shard_map.98._), channel_id=1, source_target_pairs={{0,1},{1,0},{2,3},{3,2},{4,5},{5,4},{6,7},{7,6},{8,9},{9,8},{10,11... | collective-permute-start | bytes 294920 | tf_op jit(solution)/shard_map/ppermute | solution.py:40
  52.0 13.4 %collective-permute-start.9 = (bf16[3,2,32,1024]{3,2,1,0:T(8,128)(2,1)S(1)}, bf16[3,2,32,1024]{3,2,1,0:T(8,128)(2,1)S(1)}, u32[]{:S(2)}, u32[]{:S(2)}) collective-permute-start(bf16[3,2,32,1024]{3,2,1,0:T(8,128)(2,1)S(1)} %get-tuple-element.20.refs_0_), channel_id=1, source_target_pairs={{0,8},{8,0},{16,24},{24,16},{1,9},{9,1},{17,25},{25,17},{2,10},{10... | collective-permute-start | bytes 1179656 | tf_op jit(solution)/shard_map/ppermute | solution.py:40
  58.7 8.3 %collective-permute-start.10 = (bf16[3,2,32,1024]{3,2,1,0:T(8,128)(2,1)S(1)}, bf16[3,2,32,1024]{3,2,1,0:T(8,128)(2,1)}, u32[]{:S(2)}, u32[]{:S(2)}) collective-permute-start(bf16[3,2,32,1024]{3,2,1,0:T(8,128)(2,1)S(1)} %collective-permute-done.8.refs_0_.refs_1_), channel_id=1, source_target_pairs={{0,8},{8,0},{16,24},{24,16},{1,9},{9,1},{17,25},{25,17},{2,10},{10... | collective-permute-start | bytes 1179656 | tf_op jit(solution)/shard_map/ppermute | solution.py:40
  58.8 5.3 %collective-permute-start.14 = (bf16[384,128]{1,0:T(8,128)(2,1)S(1)}, bf16[384,128]{1,0:T(8,128)(2,1)S(1)}, u32[]{:S(2)}, u32[]{:S(2)}) collective-permute-start(bf16[384,128]{1,0:T(8,128)(2,1)S(1)} %add_convert_fusion.refs_4_), channel_id=1, source_target_pairs={{0,16},{8,24},{16,0},{24,8},{1,17},{9,25},{17,1},{25,9},{2,18},{10... | collective-permute-start | bytes 294920 | tf_op jit(solution)/shard_map/ppermute | solution.py:40
  60.4 3.7 %collective-permute-start.15 = (bf16[384,128]{1,0:T(8,128)(2,1)S(1)}, bf16[384,128]{1,0:T(8,128)(2,1)S(1)}, u32[]{:S(2)}, u32[]{:S(2)}) collective-permute-start(bf16[384,128]{1,0:T(8,128)(2,1)S(1)} %add_convert_fusion.refs_4_), channel_id=1, source_target_pairs={{0,8},{8,0},{16,24},{24,16},{1,9},{9,1},{17,25},{25,17},{2,10},{10... | collective-permute-start | bytes 294920 | tf_op jit(solution)/shard_map/ppermute | solution.py:40
  71.7 22.0 %all-to-all-start.2 = ((bf16[8,288,128]{2,1,0:T(8,128)(2,1)}), bf16[8,288,128]{2,1,0:T(8,128)(2,1)}, u32[]{:S(2)}, u32[]{:S(2)}) async-start(bf16[8,288,128]{2,1,0:T(8,128)(2,1)} %copy-done), calls=%async_computation.2 | async-start | bytes 1179648 | tf_op jit(solution)/shard_map/all_to_all | solution.py:44
  77.4 24.8 %collective-permute-start.11 = (bf16[5,2,32,1024]{3,2,1,0:T(8,128)(2,1)}, bf16[5,2,32,1024]{3,2,1,0:T(8,128)(2,1)}, u32[]{:S(2)}, u32[]{:S(2)}) collective-permute-start(bf16[5,2,32,1024]{3,2,1,0:T(8,128)(2,1)} %copy-done.7), channel_id=1, source_target_pairs={{0,16},{8,24},{16,0},{24,8},{1,17},{9,25},{17,1},{25,9},{2,18},{10... | collective-permute-start | bytes 1966088 | tf_op jit(solution)/shard_map/ppermute | solution.py:40
  93.7 16.0 %collective-permute-start.18 = (bf16[8,288,128]{2,1,0:T(8,128)(2,1)}, bf16[8,288,128]{2,1,0:T(8,128)(2,1)}, u32[]{:S(2)}, u32[]{:S(2)}) collective-permute-start(bf16[8,288,128]{2,1,0:T(8,128)(2,1)} %all-to-all-done.2.states_ref.refs_8_), channel_id=1, source_target_pairs={{0,16},{8,24},{16,0},{24,8},{1,17},{9,25},{17,1},{25,9},{2,18},{10... | collective-permute-start | bytes 1769480 | tf_op jit(solution)/shard_map/ppermute | solution.py:40
  99.5 9.8 %all-to-all-start.3 = ((f32[32,1,128]{2,1,0:T(1,128)}), f32[32,1,128]{2,1,0:T(1,128)S(1)}, u32[]{:S(2)}, u32[]{:S(2)}) async-start(f32[32,1,128]{2,1,0:T(1,128)} %shard_map.102), calls=%async_computation.3 | async-start | bytes 32768 | tf_op jit(solution)/shard_map/all_to_all | solution.py:659
  109.2 3.2 %collective-permute-start.17 = (bf16[5,2,32,1024]{3,2,1,0:T(8,128)(2,1)}, bf16[5,2,32,1024]{3,2,1,0:T(8,128)(2,1)S(1)}, u32[]{:S(2)}, u32[]{:S(2)}) collective-permute-start(bf16[5,2,32,1024]{3,2,1,0:T(8,128)(2,1)} %shard_map.103.refs_5_), channel_id=1, source_target_pairs={{0,8},{8,0},{16,24},{24,16},{1,9},{9,1},{17,25},{25,17},{2,10},{10... | collective-permute-start | bytes 1966088 | tf_op jit(solution)/shard_map/ppermute | solution.py:40
  109.2 3.1 %collective-permute-start.19 = (bf16[8,288,128]{2,1,0:T(8,128)(2,1)}, bf16[8,288,128]{2,1,0:T(8,128)(2,1)S(1)}, u32[]{:S(2)}, u32[]{:S(2)}) collective-permute-start(bf16[8,288,128]{2,1,0:T(8,128)(2,1)} %all-to-all-done.2.states_ref.refs_8_), channel_id=1, source_target_pairs={{0,8},{8,0},{16,24},{24,16},{1,9},{9,1},{17,25},{25,17},{2,10},{10... | collective-permute-start | bytes 1769480 | tf_op jit(solution)/shard_map/ppermute | solution.py:40
  109.8 3.5 %collective-permute-start.20 = (bf16[8,288,128]{2,1,0:T(8,128)(2,1)}, bf16[8,288,128]{2,1,0:T(8,128)(2,1)S(1)}, u32[]{:S(2)}, u32[]{:S(2)}) collective-permute-start(bf16[8,288,128]{2,1,0:T(8,128)(2,1)} %shard_map.104.refs_9_), channel_id=1, source_target_pairs={{0,8},{8,0},{16,24},{24,16},{1,9},{9,1},{17,25},{25,17},{2,10},{10... | collective-permute-start | bytes 1769480 | tf_op jit(solution)/shard_map/ppermute | solution.py:40
  (24 other events, 165.1 us)

commit v3 on v2

--- a/solution.py
+++ b/solution.py
@@ -206,16 +206,20 @@
 
 
 def notes_kernel(
-    copies, slices_ref, h_ref, users_ref, included_ref, _, one_ref, two_ref, notes_ref, h_held, sem
+    copies, slices_ref, h_ref, users_ref, included_ref, _, one_ref, two_ref, notes_far, h_held, notes_ref, sems
 ):
     share, rows, _ = h_held.shape
     users = included_ref.shape[1]
     first = first_micro(copies, share)
-    copy = pltpu.make_async_copy(h_ref.at[pl.ds(first, share)], h_held, sem)
+    copy = pltpu.make_async_copy(h_ref.at[pl.ds(first, share)], h_held, sems.at[0])
     copy.start()
-    cut = one_ref.shape[0]
-    one_ref[...] = slices_ref[:cut]
-    two_ref[...] = slices_ref[cut:]
+    cut, others = one_ref.shape[0], two_ref.shape[0]
+    leaving = [
+        pltpu.make_async_copy(slices_ref.at[pl.ds(0, cut)], one_ref, sems.at[1]),
+        pltpu.make_async_copy(slices_ref.at[pl.ds(cut, others)], two_ref, sems.at[2]),
+    ]
+    for move in leaving:
+        move.start()
     copy.wait()
     lane = lax.broadcasted_iota(jnp.int32, (rows, LANES), 1)
     diagonal = lax.broadcasted_iota(jnp.int32, (rows, rows), 0) == lax.broadcasted_iota(
@@ -233,22 +237,39 @@
         notes = jnp.where(lane == 0, column.astype(F32), 0.0)
         notes = jnp.where(lane == 1, chosen.astype(F32), notes)
         notes_ref[m * rows : (m + 1) * rows, :] = jnp.where(lane == 2, square, notes)
+    leaving.append(pltpu.make_async_copy(notes_ref, notes_far, sems.at[3]))
+    leaving[-1].start()
+    for move in leaving:
+        move.wait()
+
+
+def add_far_kernel(one_ref, two_ref, out_ref, held_ref, sem):
+    held_ref[...] = (one_ref[...].astype(F32) + two_ref[...].astype(F32)).astype(BF16)
+    copy = pltpu.make_async_copy(held_ref, out_ref, sem)
+    copy.start()
+    copy.wait()
 
 
 def add_kernel(one_ref, two_ref, _, out_ref):
     out_ref[...] = (one_ref[...].astype(F32) + two_ref[...].astype(F32)).astype(BF16)
 
 
-def project_kernel(slices_ref, packs_ref, _, out_ref, token_ref):
+def project_kernel(slices_ref, packs_ref, _, out_ref, token_ref, held_ref, sems):
     token_ref[...] = jnp.zeros_like(token_ref)
     parts, _, own, slab = slices_ref.shape
     sections, _, rank = packs_ref.shape
     slice_h = slices_ref[:, 0].reshape(parts * own, slab)
     slice_c = slices_ref[:, 1].reshape(parts * own, slab)
 
+    leaving = []
+
     def put(value, index):
-        here = slice(index * own, (index + 1) * own)
-        out_ref[:, here, :] = value.astype(BF16).reshape(parts, own, rank)
+        here = pl.ds(index * own, own)
+        held_ref[:, here, :] = value.astype(BF16).reshape(parts, own, rank)
+        leaving.append(
+            pltpu.make_async_copy(held_ref.at[:, here, :], out_ref.at[:, here, :], sems.at[index])
+        )
+        leaving[-1].start()
 
     for l in range(sections):
         put(dot(slice_h, down_of(packs_ref, l, slab)), l)
@@ -257,10 +278,12 @@
         put(dot_last(slice_c, up), 2 * sections - 1 + l)
         if l < sections - 1:
             put(dot_last(slice_h, up), sections + l)
+    for move in leaving:
+        move.wait()
 
 
 def solve_kernel(width, notes_far, payload_ref, *refs):
-    *pieces, out_ref, gram_ref, notes_ref, sems = refs
+    *pieces, out_ref, gram_ref, notes_ref, held_ref, sems, out_sems = refs
     own = notes_ref.shape[0]
     parts, size, rank = out_ref.shape
     layers = (size // own - 1) // 2
@@ -276,9 +299,15 @@
     def column(index):
         return jnp.sum(payload_ref[:, index * own : (index + 1) * own, :].astype(F32), 0)
 
+    leaving = []
+
     def put(value, index):
-        here = slice(index * own, (index + 1) * own)
-        out_ref[:, here, :] = jnp.broadcast_to(value[None], (parts, own, rank))
+        here = pl.ds(index * own, own)
+        held_ref[:, here, :] = jnp.broadcast_to(value[None], (parts, own, rank))
+        leaving.append(
+            pltpu.make_async_copy(held_ref.at[:, here, :], out_ref.at[:, here, :], out_sems.at[index])
+        )
+        leaving[-1].start()
 
     p = [column(i) for i in range(layers)]
     through = [column(layers + i) for i in range(layers - 1)]
@@ -323,6 +352,8 @@
         extra = jnp.where(lane == l, coarse, extra)
         extra = jnp.where(lane == layers + l, alpha - coarse, extra)
     put(extra.astype(BF16), 2 * layers)
+    for move in leaving:
+        move.wait()
 
 
 def spread(extra, columns):
@@ -611,11 +642,22 @@
         project_kernel,
         [((parts, (3 * layers - 1) * own, rank), BF16), ((8, LANES), F32)],
         [VMEM, VMEM, ANY],
+        out_specs=[FAR, VMEM],
+        scratch_shapes=[
+            pltpu.VMEM((parts, (3 * layers - 1) * own, rank), BF16),
+            pltpu.SemaphoreType.DMA((3 * layers - 1,)),
+        ],
     )(slices, *in_vmem(packs), sent)
     payload = exchange(payload)
-    gram = (sent.astype(F32) + came.astype(F32)).astype(BF16)
+    (gram,) = call(
+        add_far_kernel,
+        [(sent.shape, BF16)],
+        [VMEM] * 2,
+        out_specs=[FAR],
+        scratch_shapes=[pltpu.VMEM(sent.shape, BF16), pltpu.SemaphoreType.DMA],
+    )(sent, came)
     grams = gather(gram)
-    cut = max(1, parts * 3 // 8)
+    cut = max(1, parts * 2 // 8)
     one, two, notes = call(
         functools.partial(notes_kernel, copies),
         [
@@ -624,23 +666,31 @@
             ((own, LANES), F32),
         ],
         [VMEM, FAR, VMEM, VMEM, VMEM],
-        scratch_shapes=[pltpu.VMEM((share, rows, width), BF16), pltpu.SemaphoreType.DMA],
+        out_specs=[FAR] * 3,
+        scratch_shapes=[
+            pltpu.VMEM((share, rows, width), BF16),
+            pltpu.VMEM((own, LANES), F32),
+            pltpu.SemaphoreType.DMA((4,)),
+        ],
     )(slices, *in_hbm(hidden_in), user_of_row, included, token)
-    ones = gather(one, copies)
+    ones = gather_far(one, copies)
     twos = gather_far(two, copies)
-    twos_own = swap(two, "section", copies)
-    count = len(ones)
+    ones_own, twos_own = swap(one, "section", copies), swap(two, "section", copies)
+    count = 2 * len(ones)
 
     (state,) = call(
         functools.partial(solve_kernel, width),
         [((parts, (2 * layers + 1) * own, rank), BF16)],
-        [FAR, VMEM] + [FAR] * (count + len(grams)),
+        [FAR, VMEM] + [FAR] * (3 + len(grams)),
         scratch_shapes=[
             pltpu.VMEM((layers * each, rank), BF16),
             pltpu.VMEM((own, LANES), F32),
+            pltpu.VMEM((parts, (2 * layers + 1) * own, rank), BF16),
             pltpu.SemaphoreType.DMA((layers + 1,)),
+            pltpu.SemaphoreType.DMA((2 * layers + 1,)),
         ],
-    )(*in_hbm(notes), payload, *in_hbm(*ones[1:], twos_own, *grams))
+        out_specs=[FAR],
+    )(*in_hbm(notes), payload, *in_hbm(ones[1], ones_own, twos_own, *grams))
     states = exchange(state)
 
     lanes = -(-users * parts // LANES) * LANES
@@ -657,7 +707,9 @@
     )(slices, *in_vmem(packs), *in_hbm(states))
     states_far = gather_far(states, copies)
     ghosts = lax.all_to_all(ghosts, ("section", "dp"), 0, 0, tiled=True)
+    ones = ones[:1] + [tie(piece, ghosts) for piece in ones[1:]]
     twos = twos[:1] + [tie(piece, ghosts) for piece in twos[1:]]
+    ones = ones + [ones_own] + [swap(piece, "section", copies) for piece in ones[1:]]
     twos = twos + [twos_own] + [swap(piece, "section", copies) for piece in twos[1:]]
     states = states_far[:1] + [tie(piece, ghosts) for piece in states_far[1:]]
     states = states + [swap(piece, "section", copies) for piece in states]

time: 120 us -> 123 us (1.025)
  Pallas kernels: 24.3 us -> 27.6 us
    pallas_call x1, Pallas kernels: 1.63 us -> 4.4 us  [shards(): call(project_kernel, [((parts, (3 * layers - 1) * own, rank), BF16), ((8,...]
    ppermute x21, waiting for transfers between devices: 29.1 us -> 27.6 us  [swap(): return lax.ppermute(block, axis, [(i, i ^ bit) for i in range(size)])]
    unnamed x47 -> x51, local copies, waits for them, and re-layouts: 4.87 us -> 4.01 us
  transfers between devices with their start and end apart: 25 -> 25, of which waited for: 11 -> 13; matrix products, arithmetic and copies ran while one was open for 0% -> 0% of each run, Pallas kernels for 8% -> 8%
where the time goes in v3:
time: 123 us
  waiting for transfers between devices  50.9 us (41%)
  starting transfers between devices  39.2 us (32%)
  Pallas kernels  27.6 us (22%)
  local copies, waits for them, and re-layouts  4.01 us (3%)
    ppermute x21, waiting for transfers between devices, swap(): return lax.ppermute(block, axis, [(i, i ^ bit) for i in range(size)])  27.6 us
    ppermute x21, starting transfers between devices, swap(): return lax.ppermute(block, axis, [(i, i ^ bit) for i in range(size)])  18.9 us
    all_to_all x3, starting transfers between devices, exchange(): return lax.all_to_all(blocks, 'dp', 0, 0, tiled=True)  17.6 us
    all_to_all x3, waiting for transfers between devices, exchange(): return lax.all_to_all(blocks, 'dp', 0, 0, tiled=True)  15.7 us
    all_to_all x1, waiting for transfers between devices, shards(): ghosts = lax.all_to_all(ghosts, ('section', 'dp'), 0, 0, tiled=True)  7.62 us
    pallas_call x1, Pallas kernels, shards(): call(functools.partial(grads_kernel, rows, users, bound, copies), [((1, s...  6.4 us
    pallas_call x1, Pallas kernels, shards(): call(project_kernel, [((parts, (3 * layers - 1) * own, rank), BF16), ((8,...  4.4 us
    pallas_call x1, Pallas kernels, shards(): call(functools.partial(streams_kernel, rows, users), [((sections * parts,...  4.22 us
  transfers between devices with their start and end apart: 25, of which 13 were waited for; matrix products, arithmetic and copies ran while one was open for 0% of the time, Pallas kernels for 8%

profile of v3, /device:TPU:0, one launch (start us, length us, event | category | flops | bytes accessed | tf_op | source)
XLA Modules:
  0.0 122.8 jit_solution(17481597676639981977)
XLA Ops:
  0.6 2.4 %shard_map.96 = bf16[8,2,32,1024]{3,2,1,0:T(8,128)(2,1)} custom-call(bf16[4,32,8192]{2,1,0:T(8,128)(2,1)} %h_ref.3, bf16[4,32,8192]{2,1,0:T(8,128)(2,1)} %c_ref.1), custom_call_target="tpu_custom_call" | custom-call | tf_op jit(solution)/shard_map/pallas_call | solution.py:614
  3.1 7.3 %all-to-all-start = ((bf16[8,2,32,1024]{3,2,1,0:T(8,128)(2,1)}), bf16[8,2,32,1024]{3,2,1,0:T(8,128)(2,1)S(1)}, u32[]{:S(2)}, u32[]{:S(2)}) async-start(bf16[8,2,32,1024]{3,2,1,0:T(8,128)(2,1)} %shard_map.96), calls=%async_computation | async-start | bytes 2097152 | tf_op jit(solution)/shard_map/all_to_all | solution.py:44
  11.6 1.6 %collective-permute-start = (bf16[1024,128]{1,0:T(8,128)(2,1)S(1)}, bf16[1024,128]{1,0:T(8,128)(2,1)S(1)}, u32[]{:S(2)}, u32[]{:S(2)}) collective-permute-start(bf16[1024,128]{1,0:T(8,128)(2,1)S(1)} %get-tuple-element.15.refs_0_), channel_id=1, source_target_pairs={{0,16},{8,24},{16,0},{24,8},{1,17},{9,25},{17,1},{25,9},{2,18},{10... | collective-permute-start | bytes 786440 | tf_op jit(solution)/shard_map/ppermute | solution.py:40
  13.2 6.2 %collective-permute-done.refs_1_ = bf16[1024,128]{1,0:T(8,128)(2,1)S(1)} collective-permute-done((bf16[1024,128]{1,0:T(8,128)(2,1)S(1)}, bf16[1024,128]{1,0:T(8,128)(2,1)S(1)}, u32[]{:S(2)}, u32[]{:S(2)}) %collective-permute-start) | collective-permute-done | bytes 262176 | tf_op jit(solution)/shard_map/ppermute | solution.py:40
  21.0 1.7 %shard_map.97 = bf16[384,128]{1,0:T(8,128)(2,1)S(1)} custom-call(bf16[1040,128]{1,0:T(8,128)(2,1)S(1)} %get-tuple-element.16.refs_4_.down_ref, bf16[1024,128]{1,0:T(8,128)(2,1)} %copy-done.5, bf16[1024,128]{1,0:T(8,128)(2,1)S(1)} %collective-permute-done.refs_1_, bf16[1024,128]{1,0:T(8,128)(2,1)S(1)} %collective-permute-done.1.refs_2_, ...), custom_call_target="tpu_custom_call" | custom-call | tf_op jit(solution)/shard_map/pallas_call | solution.py:623
  22.8 1.8 %collective-permute-start.6 = (bf16[384,128]{1,0:T(8,128)(2,1)S(1)}, bf16[384,128]{1,0:T(8,128)(2,1)S(1)}, u32[]{:S(2)}, u32[]{:S(2)}) collective-permute-start(bf16[384,128]{1,0:T(8,128)(2,1)S(1)} %shard_map.97), channel_id=1, source_target_pairs={{0,2},{1,3},{2,0},{3,1},{4,6},{5,7},{6,4},{7,5},{8,10},{9,11},{10,... | collective-permute-start | bytes 294920 | tf_op jit(solution)/shard_map/ppermute | solution.py:40
  24.6 3.7 %collective-permute-done.3.refs_5_ = bf16[1040,128]{1,0:T(8,128)(2,1)S(1)} collective-permute-done((bf16[1040,128]{1,0:T(8,128)(2,1)S(1)}, bf16[1040,128]{1,0:T(8,128)(2,1)S(1)}, u32[]{:S(2)}, u32[]{:S(2)}) %collective-permute-start.3) | collective-permute-done | bytes 266272 | tf_op jit(solution)/shard_map/ppermute | solution.py:40
  29.5 4.6 %collective-permute-start.7 = (bf16[384,128]{1,0:T(8,128)(2,1)S(1)}, bf16[384,128]{1,0:T(8,128)(2,1)S(1)}, u32[]{:S(2)}, u32[]{:S(2)}) collective-permute-start(bf16[384,128]{1,0:T(8,128)(2,1)S(1)} %add_convert_fusion.one_ref), channel_id=1, source_target_pairs={{0,4},{1,5},{2,6},{3,7},{4,0},{5,1},{6,2},{7,3},{8,12},{9,13},{10,... | collective-permute-start | bytes 294920 | tf_op jit(solution)/shard_map/ppermute | solution.py:40
  35.6 1.6 %shard_map.95 = (bf16[4,2064,128]{2,1,0:T(8,128)(2,1)S(1)}, f32[8,128]{1,0:T(8,128)S(1)}) custom-call(bf16[1024,128]{1,0:T(8,128)(2,1)} %copy-done.5, bf16[1024,128]{1,0:T(8,128)(2,1)} %copy-done.6, bf16[1024,128]{1,0:T(8,128)(2,1)} %copy-done.7, bf16[1024,128]{1,0:T(8,128)(2,1)} %copy-done.8, bf16[1040,128]{1,0:T(8,128)(2,1)} %copy-done.4, ...), custom_call_target="tpu_custom_call" | custom-call | tf_op jit(solution)/shard_map/pallas_call | solution.py:632
  37.2 3.1 %collective-permute-done.7.two_ref = bf16[384,128]{1,0:T(8,128)(2,1)S(1)} collective-permute-done((bf16[384,128]{1,0:T(8,128)(2,1)S(1)}, bf16[384,128]{1,0:T(8,128)(2,1)S(1)}, u32[]{:S(2)}, u32[]{:S(2)}) %collective-permute-start.7) | collective-permute-done | bytes 98336 | tf_op jit(solution)/shard_map/ppermute | solution.py:40
  40.4 4.4 %shard_map.99 = (bf16[8,352,128]{2,1,0:T(8,128)(2,1)S(1)}, f32[8,128]{1,0:T(8,128)S(1)}) custom-call(bf16[8,2,32,1024]{3,2,1,0:T(8,128)(2,1)S(1)} %all-to-all-done.slices_ref, bf16[4,2064,128]{2,1,0:T(8,128)(2,1)S(1)} %get-tuple-element.17.packs_ref, bf16[384,128]{1,0:T(8,128)(2,1)S(1)} %shard_map.98._.one_ref), custom_call_target="tpu_custom_call" | custom-call | tf_op jit(solution)/shard_map/pallas_call | solution.py:641
  45.6 4.2 %all-to-all-start.1 = ((bf16[8,352,128]{2,1,0:T(8,128)(2,1)}), bf16[8,352,128]{2,1,0:T(8,128)(2,1)}, u32[]{:S(2)}, u32[]{:S(2)}) async-start(bf16[8,352,128]{2,1,0:T(8,128)(2,1)} %copy-done.10), calls=%async_computation.1 | async-start | bytes 1441792 | tf_op jit(solution)/shard_map/all_to_all | solution.py:44
  51.4 2.0 %collective-permute-start.11 = (bf16[384,128]{1,0:T(8,128)(2,1)S(1)}, bf16[384,128]{1,0:T(8,128)(2,1)S(1)}, u32[]{:S(2)}, u32[]{:S(2)}) collective-permute-start(bf16[384,128]{1,0:T(8,128)(2,1)S(1)} %shard_map.98._.one_ref), channel_id=1, source_target_pairs={{0,1},{1,0},{2,3},{3,2},{4,5},{5,4},{6,7},{7,6},{8,9},{9,8},{10,11... | collective-permute-start | bytes 294920 | tf_op jit(solution)/shard_map/ppermute | solution.py:40
  55.1 5.4 %collective-permute-done.11.two_ref = bf16[384,128]{1,0:T(8,128)(2,1)S(1)} collective-permute-done((bf16[384,128]{1,0:T(8,128)(2,1)S(1)}, bf16[384,128]{1,0:T(8,128)(2,1)S(1)}, u32[]{:S(2)}, u32[]{:S(2)}) %collective-permute-start.11) | collective-permute-done | bytes 98336 | tf_op jit(solution)/shard_map/ppermute | solution.py:40
  60.6 1.6 %collective-permute-start.12 = (bf16[384,128]{1,0:T(8,128)(2,1)S(1)}, bf16[384,128]{1,0:T(8,128)(2,1)S(1)}, u32[]{:S(2)}, u32[]{:S(2)}) collective-permute-start(bf16[384,128]{1,0:T(8,128)(2,1)S(1)} %shard_map.101.refs_3_), channel_id=1, source_target_pairs={{0,16},{8,24},{16,0},{24,8},{1,17},{9,25},{17,1},{25,9},{2,18},{10... | collective-permute-start | bytes 294920 | tf_op jit(solution)/shard_map/ppermute | solution.py:40
  62.2 3.1 %collective-permute-done.12.refs_4_ = bf16[384,128]{1,0:T(8,128)(2,1)S(1)} collective-permute-done((bf16[384,128]{1,0:T(8,128)(2,1)S(1)}, bf16[384,128]{1,0:T(8,128)(2,1)S(1)}, u32[]{:S(2)}, u32[]{:S(2)}) %collective-permute-start.12) | collective-permute-done | bytes 98336 | tf_op jit(solution)/shard_map/ppermute | solution.py:40
  68.3 4.1 %shard_map.102 = bf16[8,288,128]{2,1,0:T(8,128)(2,1)S(1)} custom-call(f32[32,128]{1,0:T(8,128)} %copy-done.13, bf16[8,352,128]{2,1,0:T(8,128)(2,1)} %all-to-all-done.1.payload_ref, bf16[2,2,32,1024]{3,2,1,0:T(8,128)(2,1)} %copy-done, bf16[2,2,32,1024]{3,2,1,0:T(8,128)(2,1)} %copy-done.16, bf16[6,2,32,1024]{3,2,1,0:T(8,128)(2,1)} %collective-permute-done.10.refs_2_.refs_6_, ...), custom_call_target="tpu_custom_call" | custom-call | tf_op jit(solution)/shard_map/pallas_call | solution.py:681
  73.2 6.1 %all-to-all-start.2 = ((bf16[8,288,128]{2,1,0:T(8,128)(2,1)}), bf16[8,288,128]{2,1,0:T(8,128)(2,1)}, u32[]{:S(2)}, u32[]{:S(2)}) async-start(bf16[8,288,128]{2,1,0:T(8,128)(2,1)} %copy-done.3), calls=%async_computation.2 | async-start | bytes 1179648 | tf_op jit(solution)/shard_map/all_to_all | solution.py:44
  80.8 14.8 %all-to-all-done.2.states_ref.refs_8_ = bf16[8,288,128]{2,1,0:T(8,128)(2,1)} async-done(((bf16[8,288,128]{2,1,0:T(8,128)(2,1)}), bf16[8,288,128]{2,1,0:T(8,128)(2,1)}, u32[]{:S(2)}, u32[]{:S(2)}) %all-to-all-start.2) | async-done | bytes 589856 | tf_op jit(solution)/shard_map/all_to_all | solution.py:44
  97.1 4.2 %shard_map.103 = f32[32,1,128]{2,1,0:T(1,128)} custom-call(bf16[8,2,32,1024]{3,2,1,0:T(8,128)(2,1)S(1)} %all-to-all-done.slices_ref, bf16[4,2064,128]{2,1,0:T(8,128)(2,1)S(1)} %get-tuple-element.17.packs_ref, bf16[8,288,128]{2,1,0:T(8,128)(2,1)} %all-to-all-done.2.states_ref.refs_8_), custom_call_target="tpu_custom_call" | custom-call | tf_op jit(solution)/shard_map/pallas_call | solution.py:697
  101.4 2.7 %all-to-all-start.3 = ((f32[32,1,128]{2,1,0:T(1,128)}), f32[32,1,128]{2,1,0:T(1,128)S(1)}, u32[]{:S(2)}, u32[]{:S(2)}) async-start(f32[32,1,128]{2,1,0:T(1,128)} %shard_map.103), calls=%async_computation.3 | async-start | bytes 32768 | tf_op jit(solution)/shard_map/all_to_all | solution.py:709
  104.1 7.6 %all-to-all-done.3._ = f32[32,1,128]{2,1,0:T(1,128)S(1)} async-done(((f32[32,1,128]{2,1,0:T(1,128)}), f32[32,1,128]{2,1,0:T(1,128)S(1)}, u32[]{:S(2)}, u32[]{:S(2)}) %all-to-all-start.3) | async-done | bytes 16416 | tf_op jit(solution)/shard_map/all_to_all | solution.py:709
  112.8 2.0 %collective-permute-done.15.refs_3_ = bf16[2,2,32,1024]{3,2,1,0:T(8,128)(2,1)S(1)} collective-permute-done((bf16[2,2,32,1024]{3,2,1,0:T(8,128)(2,1)S(1)}, bf16[2,2,32,1024]{3,2,1,0:T(8,128)(2,1)S(1)}, u32[]{:S(2)}, u32[]{:S(2)}) %collective-permute-start.15) | collective-permute-done | bytes 262176 | tf_op jit(solution)/shard_map/ppermute | solution.py:40
  116.4 6.4 %shard_map.107 = (f32[1,1024,128]{2,1,0:T(8,128)}, f32[1,128,1024]{2,1,0:T(8,128)}, f32[2,4]{1,0:T(2,128)}) custom-call(bf16[4,2064,128]{2,1,0:T(8,128)(2,1)S(1)} %get-tuple-element.17.packs_ref, bf16[2,2,32,1024]{3,2,1,0:T(8,128)(2,1)} %copy-done.12, bf16[2,2,32,1024]{3,2,1,0:T(8,128)(2,1)} %copy-done.2, bf16[2,2,32,1024]{3,2,1,0:T(8,128)(2,1)} %copy-done.16, ...), custom_call_target="tpu_custom_call" | custom-call | tf_op jit(solution)/shard_map/pallas_call | solution.py:719
  (92 shorter events, 19.1 us)
Async XLA Ops:
  3.1 37.3 %all-to-all-start = ((bf16[8,2,32,1024]{3,2,1,0:T(8,128)(2,1)}), bf16[8,2,32,1024]{3,2,1,0:T(8,128)(2,1)S(1)}, u32[]{:S(2)}, u32[]{:S(2)}) async-start(bf16[8,2,32,1024]{3,2,1,0:T(8,128)(2,1)} %shard_map.96), calls=%async_computation | async-start | bytes 2097152 | tf_op jit(solution)/shard_map/all_to_all | solution.py:44
  11.6 7.8 %collective-permute-start = (bf16[1024,128]{1,0:T(8,128)(2,1)S(1)}, bf16[1024,128]{1,0:T(8,128)(2,1)S(1)}, u32[]{:S(2)}, u32[]{:S(2)}) collective-permute-start(bf16[1024,128]{1,0:T(8,128)(2,1)S(1)} %get-tuple-element.15.refs_0_), channel_id=1, source_target_pairs={{0,16},{8,24},{16,0},{24,8},{1,17},{9,25},{17,1},{25,9},{2,18},{10... | collective-permute-start | bytes 786440 | tf_op jit(solution)/shard_map/ppermute | solution.py:40
  13.2 7.8 %collective-permute-start.1 = (bf16[1024,128]{1,0:T(8,128)(2,1)S(1)}, bf16[1024,128]{1,0:T(8,128)(2,1)S(1)}, u32[]{:S(2)}, u32[]{:S(2)}) collective-permute-start(bf16[1024,128]{1,0:T(8,128)(2,1)S(1)} %get-tuple-element.15.refs_0_), channel_id=1, source_target_pairs={{0,8},{8,0},{16,24},{24,16},{1,9},{9,1},{17,25},{25,17},{2,10},{10... | collective-permute-start | bytes 786440 | tf_op jit(solution)/shard_map/ppermute | solution.py:40
  19.5 1.5 %collective-permute-start.2 = (bf16[1024,128]{1,0:T(8,128)(2,1)S(1)}, bf16[1024,128]{1,0:T(8,128)(2,1)S(1)}, u32[]{:S(2)}, u32[]{:S(2)}) collective-permute-start(bf16[1024,128]{1,0:T(8,128)(2,1)S(1)} %collective-permute-done.refs_1_), channel_id=1, source_target_pairs={{0,8},{8,0},{16,24},{24,16},{1,9},{9,1},{17,25},{25,17},{2,10},{10... | collective-permute-start | bytes 786440 | tf_op jit(solution)/shard_map/ppermute | solution.py:40
  19.5 8.8 %collective-permute-start.3 = (bf16[1040,128]{1,0:T(8,128)(2,1)S(1)}, bf16[1040,128]{1,0:T(8,128)(2,1)S(1)}, u32[]{:S(2)}, u32[]{:S(2)}) collective-permute-start(bf16[1040,128]{1,0:T(8,128)(2,1)S(1)} %get-tuple-element.16.refs_4_.down_ref), channel_id=1, source_target_pairs={{0,16},{8,24},{16,0},{24,8},{1,17},{9,25},{17,1},{25,9},{2,18},{10... | collective-permute-start | bytes 798728 | tf_op jit(solution)/shard_map/ppermute | solution.py:40
  22.8 6.8 %collective-permute-start.6 = (bf16[384,128]{1,0:T(8,128)(2,1)S(1)}, bf16[384,128]{1,0:T(8,128)(2,1)S(1)}, u32[]{:S(2)}, u32[]{:S(2)}) collective-permute-start(bf16[384,128]{1,0:T(8,128)(2,1)S(1)} %shard_map.97), channel_id=1, source_target_pairs={{0,2},{1,3},{2,0},{3,1},{4,6},{5,7},{6,4},{7,5},{8,10},{9,11},{10,... | collective-permute-start | bytes 294920 | tf_op jit(solution)/shard_map/ppermute | solution.py:40
  24.6 9.6 %collective-permute-start.4 = (bf16[1040,128]{1,0:T(8,128)(2,1)S(1)}, bf16[1040,128]{1,0:T(8,128)(2,1)S(1)}, u32[]{:S(2)}, u32[]{:S(2)}) collective-permute-start(bf16[1040,128]{1,0:T(8,128)(2,1)S(1)} %get-tuple-element.16.refs_4_.down_ref), channel_id=1, source_target_pairs={{0,8},{8,0},{16,24},{24,16},{1,9},{9,1},{17,25},{25,17},{2,10},{10... | collective-permute-start | bytes 798728 | tf_op jit(solution)/shard_map/ppermute | solution.py:40
  28.3 5.9 %collective-permute-start.5 = (bf16[1040,128]{1,0:T(8,128)(2,1)S(1)}, bf16[1040,128]{1,0:T(8,128)(2,1)S(1)}, u32[]{:S(2)}, u32[]{:S(2)}) collective-permute-start(bf16[1040,128]{1,0:T(8,128)(2,1)S(1)} %collective-permute-done.3.refs_5_), channel_id=1, source_target_pairs={{0,8},{8,0},{16,24},{24,16},{1,9},{9,1},{17,25},{25,17},{2,10},{10... | collective-permute-start | bytes 798728 | tf_op jit(solution)/shard_map/ppermute | solution.py:40
  29.5 10.8 %collective-permute-start.7 = (bf16[384,128]{1,0:T(8,128)(2,1)S(1)}, bf16[384,128]{1,0:T(8,128)(2,1)S(1)}, u32[]{:S(2)}, u32[]{:S(2)}) collective-permute-start(bf16[384,128]{1,0:T(8,128)(2,1)S(1)} %add_convert_fusion.one_ref), channel_id=1, source_target_pairs={{0,4},{1,5},{2,6},{3,7},{4,0},{5,1},{6,2},{7,3},{8,12},{9,13},{10,... | collective-permute-start | bytes 294920 | tf_op jit(solution)/shard_map/ppermute | solution.py:40
  45.6 22.6 %all-to-all-start.1 = ((bf16[8,352,128]{2,1,0:T(8,128)(2,1)}), bf16[8,352,128]{2,1,0:T(8,128)(2,1)}, u32[]{:S(2)}, u32[]{:S(2)}) async-start(bf16[8,352,128]{2,1,0:T(8,128)(2,1)} %copy-done.10), calls=%async_computation.1 | async-start | bytes 1441792 | tf_op jit(solution)/shard_map/all_to_all | solution.py:44
  51.3 16.1 %collective-permute-start.10 = (bf16[6,2,32,1024]{3,2,1,0:T(8,128)(2,1)S(1)}, bf16[6,2,32,1024]{3,2,1,0:T(8,128)(2,1)}, u32[]{:S(2)}, u32[]{:S(2)}) collective-permute-start(bf16[6,2,32,1024]{3,2,1,0:T(8,128)(2,1)S(1)} %get-tuple-element.23.refs_4_), channel_id=1, source_target_pairs={{0,8},{8,0},{16,24},{24,16},{1,9},{9,1},{17,25},{25,17},{2,10},{10... | collective-permute-start | bytes 2359304 | tf_op jit(solution)/shard_map/ppermute | solution.py:40
  51.4 9.0 %collective-permute-start.11 = (bf16[384,128]{1,0:T(8,128)(2,1)S(1)}, bf16[384,128]{1,0:T(8,128)(2,1)S(1)}, u32[]{:S(2)}, u32[]{:S(2)}) collective-permute-start(bf16[384,128]{1,0:T(8,128)(2,1)S(1)} %shard_map.98._.one_ref), channel_id=1, source_target_pairs={{0,1},{1,0},{2,3},{3,2},{4,5},{5,4},{6,7},{7,6},{8,9},{9,8},{10,11... | collective-permute-start | bytes 294920 | tf_op jit(solution)/shard_map/ppermute | solution.py:40
  53.4 13.2 %collective-permute-start.9 = (bf16[2,2,32,1024]{3,2,1,0:T(8,128)(2,1)S(1)}, bf16[2,2,32,1024]{3,2,1,0:T(8,128)(2,1)S(1)}, u32[]{:S(2)}, u32[]{:S(2)}) collective-permute-start(bf16[2,2,32,1024]{3,2,1,0:T(8,128)(2,1)S(1)} %get-tuple-element.20.refs_0_), channel_id=1, source_target_pairs={{0,8},{8,0},{16,24},{24,16},{1,9},{9,1},{17,25},{25,17},{2,10},{10... | collective-permute-start | bytes 786440 | tf_op jit(solution)/shard_map/ppermute | solution.py:40
  53.5 13.1 %collective-permute-start.8 = (bf16[2,2,32,1024]{3,2,1,0:T(8,128)(2,1)S(1)}, bf16[2,2,32,1024]{3,2,1,0:T(8,128)(2,1)S(1)}, u32[]{:S(2)}, u32[]{:S(2)}) collective-permute-start(bf16[2,2,32,1024]{3,2,1,0:T(8,128)(2,1)S(1)} %get-tuple-element.20.refs_0_), channel_id=1, source_target_pairs={{0,16},{8,24},{16,0},{24,8},{1,17},{9,25},{17,1},{25,9},{2,18},{10... | collective-permute-start | bytes 786440 | tf_op jit(solution)/shard_map/ppermute | solution.py:40
  60.6 4.7 %collective-permute-start.12 = (bf16[384,128]{1,0:T(8,128)(2,1)S(1)}, bf16[384,128]{1,0:T(8,128)(2,1)S(1)}, u32[]{:S(2)}, u32[]{:S(2)}) collective-permute-start(bf16[384,128]{1,0:T(8,128)(2,1)S(1)} %shard_map.101.refs_3_), channel_id=1, source_target_pairs={{0,16},{8,24},{16,0},{24,8},{1,17},{9,25},{17,1},{25,9},{2,18},{10... | collective-permute-start | bytes 294920 | tf_op jit(solution)/shard_map/ppermute | solution.py:40
  62.2 3.1 %collective-permute-start.13 = (bf16[384,128]{1,0:T(8,128)(2,1)S(1)}, bf16[384,128]{1,0:T(8,128)(2,1)S(1)}, u32[]{:S(2)}, u32[]{:S(2)}) collective-permute-start(bf16[384,128]{1,0:T(8,128)(2,1)S(1)} %shard_map.101.refs_3_), channel_id=1, source_target_pairs={{0,8},{8,0},{16,24},{24,16},{1,9},{9,1},{17,25},{25,17},{2,10},{10... | collective-permute-start | bytes 294920 | tf_op jit(solution)/shard_map/ppermute | solution.py:40
  73.2 22.5 %all-to-all-start.2 = ((bf16[8,288,128]{2,1,0:T(8,128)(2,1)}), bf16[8,288,128]{2,1,0:T(8,128)(2,1)}, u32[]{:S(2)}, u32[]{:S(2)}) async-start(bf16[8,288,128]{2,1,0:T(8,128)(2,1)} %copy-done.3), calls=%async_computation.2 | async-start | bytes 1179648 | tf_op jit(solution)/shard_map/all_to_all | solution.py:44
  79.3 24.8 %collective-permute-start.16 = (bf16[6,2,32,1024]{3,2,1,0:T(8,128)(2,1)}, bf16[6,2,32,1024]{3,2,1,0:T(8,128)(2,1)}, u32[]{:S(2)}, u32[]{:S(2)}) collective-permute-start(bf16[6,2,32,1024]{3,2,1,0:T(8,128)(2,1)} %copy-done.9), channel_id=1, source_target_pairs={{0,16},{8,24},{16,0},{24,8},{1,17},{9,25},{17,1},{25,9},{2,18},{10... | collective-permute-start | bytes 2359304 | tf_op jit(solution)/shard_map/ppermute | solution.py:40
  95.6 16.6 %collective-permute-start.18 = (bf16[8,288,128]{2,1,0:T(8,128)(2,1)}, bf16[8,288,128]{2,1,0:T(8,128)(2,1)}, u32[]{:S(2)}, u32[]{:S(2)}) collective-permute-start(bf16[8,288,128]{2,1,0:T(8,128)(2,1)} %all-to-all-done.2.states_ref.refs_8_), channel_id=1, source_target_pairs={{0,16},{8,24},{16,0},{24,8},{1,17},{9,25},{17,1},{25,9},{2,18},{10... | collective-permute-start | bytes 1769480 | tf_op jit(solution)/shard_map/ppermute | solution.py:40
  101.4 10.4 %all-to-all-start.3 = ((f32[32,1,128]{2,1,0:T(1,128)}), f32[32,1,128]{2,1,0:T(1,128)S(1)}, u32[]{:S(2)}, u32[]{:S(2)}) async-start(f32[32,1,128]{2,1,0:T(1,128)} %shard_map.103), calls=%async_computation.3 | async-start | bytes 32768 | tf_op jit(solution)/shard_map/all_to_all | solution.py:709
  111.8 3.7 %collective-permute-start.17 = (bf16[6,2,32,1024]{3,2,1,0:T(8,128)(2,1)}, bf16[6,2,32,1024]{3,2,1,0:T(8,128)(2,1)S(1)}, u32[]{:S(2)}, u32[]{:S(2)}) collective-permute-start(bf16[6,2,32,1024]{3,2,1,0:T(8,128)(2,1)} %shard_map.105.refs_5_), channel_id=1, source_target_pairs={{0,8},{8,0},{16,24},{24,16},{1,9},{9,1},{17,25},{25,17},{2,10},{10... | collective-permute-start | bytes 2359304 | tf_op jit(solution)/shard_map/ppermute | solution.py:40
  111.8 3.6 %collective-permute-start.19 = (bf16[8,288,128]{2,1,0:T(8,128)(2,1)}, bf16[8,288,128]{2,1,0:T(8,128)(2,1)S(1)}, u32[]{:S(2)}, u32[]{:S(2)}) collective-permute-start(bf16[8,288,128]{2,1,0:T(8,128)(2,1)} %all-to-all-done.2.states_ref.refs_8_), channel_id=1, source_target_pairs={{0,8},{8,0},{16,24},{24,16},{1,9},{9,1},{17,25},{25,17},{2,10},{10... | collective-permute-start | bytes 1769480 | tf_op jit(solution)/shard_map/ppermute | solution.py:40
  112.3 4.0 %collective-permute-start.20 = (bf16[8,288,128]{2,1,0:T(8,128)(2,1)}, bf16[8,288,128]{2,1,0:T(8,128)(2,1)S(1)}, u32[]{:S(2)}, u32[]{:S(2)}) collective-permute-start(bf16[8,288,128]{2,1,0:T(8,128)(2,1)} %shard_map.106.refs_9_), channel_id=1, source_target_pairs={{0,8},{8,0},{16,24},{24,16},{1,9},{9,1},{17,25},{25,17},{2,10},{10... | collective-permute-start | bytes 1769480 | tf_op jit(solution)/shard_map/ppermute | solution.py:40
  112.4 2.4 %collective-permute-start.15 = (bf16[2,2,32,1024]{3,2,1,0:T(8,128)(2,1)S(1)}, bf16[2,2,32,1024]{3,2,1,0:T(8,128)(2,1)S(1)}, u32[]{:S(2)}, u32[]{:S(2)}) collective-permute-start(bf16[2,2,32,1024]{3,2,1,0:T(8,128)(2,1)S(1)} %shard_map.104.refs_1_), channel_id=1, source_target_pairs={{0,8},{8,0},{16,24},{24,16},{1,9},{9,1},{17,25},{25,17},{2,10},{10... | collective-permute-start | bytes 786440 | tf_op jit(solution)/shard_map/ppermute | solution.py:40
  (26 other events, 178.4 us)
